TPU v7x, 32 devices: a whole 2x2x4 slice. The times are simulated.
32 devices in a mesh: tok: 16 (over z, y, x), ch: 2 (over core).
Axes of the slice: x: 2, y: 2, z: 4, core: 2. Of those that a mesh axis runs over, the one named last changes fastest.
Arguments:
- hidden: bfloat16 [2048, 1024], P('tok'), may hold values from -13 to 13
- pre_gates: bfloat16 [2, 2048, 1024], P(None, 'tok', 'ch'), may hold values from -6 to 6
- conv_weight: bfloat16 [2, 4, 1024, 1024], P(None, None, 'tok', 'ch'), may hold values from -0.09375 to 0.09375
- head_weight: bfloat16 [1024, 20480], P('tok', 'ch'), may hold values from -8 to 8
- cluster_weight: bfloat16 [1024, 32], P('tok', 'ch'), may hold values from -0.59765625 to 0.59765625
- tail1_proj: bfloat16 [16, 1024, 256], P('tok'), may hold values from -1 to 1
- tail2_proj: bfloat16 [16, 1024, 64], P('tok'), may hold values from -1 to 1
- tail1_out: bfloat16 [16, 256, 3072], P('tok', None, 'ch'), may hold values from -12 to 12
- tail2_out: bfloat16 [16, 64, 9216], P('tok', None, 'ch'), may hold values from -30 to 30
- cluster_id: int32 [2048], P('tok'), may hold values from -1 to 31, as said below
- target: int32 [2048], P('tok'), may hold values from 0 to 20479, as said below
Outputs:
- token_loss: float32 [2048], P('tok')
- grad_input: bfloat16 [2048, 1024], P('tok', 'ch')
- proj1_grad: float32 [16, 1024, 256], P('tok', 'ch')
- proj2_grad: float32 [16, 1024, 64], P('tok', 'ch')
- out1_grad: float32 [16, 256, 3072], P('tok', None, 'ch')
- out2_grad: float32 [16, 64, 9216], P('tok', None, 'ch')
Inputs may be any that keep to these rules, and one draw needn't show every extreme that they name: `cluster_id`: in each aligned block of 128 tokens at most 8 name clusters of one owner; in every draw one owner is named by 8 tokens of every block, and every owner by 8 tokens of some block. `target`: below 20480 for a head token, below 3072 for a first-tier token, below 9216 for a second-tier token.
All inputs are finite; a program needn't handle non-finite values.
Results may differ from a plain program's by a relative error of at most 0.01.
Values may be sent and summed in bfloat16 or wider, within the bound.
A program may use at most 128 MiB of HBM per device.

v0:
```python
import jax
import jax.numpy as jnp
from jax import lax
from jax.sharding import PartitionSpec as P

K = 4
LEN = 128


def merged(x, axis, combine):
    everything = jax.tree.map(lambda part: lax.all_gather(part, axis), x)
    first = jax.tree.map(lambda part: part[0], everything)

    def hop(k, so_far):
        return combine(so_far, jax.tree.map(lambda part: part[k], everything))

    return lax.fori_loop(1, lax.axis_size(axis), hop, first)


def softmax_parts(logits):
    row_max = jnp.max(logits, axis=1)
    expo_terms = jnp.exp(logits - row_max[:, None])
    return (row_max, jnp.sum(expo_terms, axis=1), expo_terms.astype(jnp.bfloat16))


def joined(left_side, right_side):
    merged_max = jnp.maximum(left_side[0], right_side[0])
    left_scale = jnp.exp(left_side[0] - merged_max)
    right_scale = jnp.exp(right_side[0] - merged_max)
    merged_sum = left_side[1] * left_scale + right_side[1] * right_scale
    if len(left_side) == 5:
        merged_value = left_side[2] * left_scale[:, None] + right_side[2] * right_scale[:, None]
        return (
            merged_max,
            merged_sum,
            merged_value,
            left_side[3] + right_side[3],
            left_side[4] + right_side[4],
        )
    return (merged_max, merged_sum, left_side[2] + right_side[2])


def joined_all(left_side, right_side):
    return tuple(
        (joined(left_group, right_group) for left_group, right_group in zip(left_side, right_side))
    )


def tier_local(features, word_ids, member, out_shard, ch_index):
    out_width = out_shard.shape[1]
    logits = jnp.dot(features, out_shard, preferred_element_type=jnp.float32)
    row_max, row_sum, weights = softmax_parts(logits)
    row_value = jnp.dot(weights, out_shard.T, preferred_element_type=jnp.float32)
    local_col = word_ids - ch_index * out_width
    inside = member & (local_col >= 0) & (local_col < out_width)
    column = jnp.clip(local_col, 0, out_width - 1)
    picked = jnp.take_along_axis(logits, column[:, None], axis=1)[:, 0]
    target_logit = jnp.where(inside, picked, 0.0)
    column_value = jnp.take(out_shard, column, axis=1).T.astype(jnp.float32)
    target_value = jnp.where(inside[:, None], column_value, 0.0)
    return (logits, inside, column, (row_max, row_sum, row_value, target_value, target_logit))


def tier_finish(features, logits, inside, column, member, totals, rows_part, proj_part):
    merged_max, merged_sum, merged_value, target_value, target_logit = totals
    log_total = merged_max + jnp.log(merged_sum)
    tail_dz = jnp.where(
        member[:, None], merged_value / merged_sum[:, None] - target_value, 0.0
    ).astype(jnp.bfloat16)
    probability = jnp.exp(logits - log_total[:, None])
    positions = jnp.arange(logits.shape[1], dtype=jnp.int32)
    target_hot = ((positions[None, :] == column[:, None]) & inside[:, None]).astype(jnp.float32)
    dlogit = jnp.where(member[:, None], probability - target_hot, 0.0).astype(jnp.bfloat16)
    out_grad = jnp.einsum("sp,sw->pw", features, dlogit, preferred_element_type=jnp.float32)
    proj_grad = jnp.einsum("sd,sp->dp", rows_part, tail_dz, preferred_element_type=jnp.float32)
    returned = jnp.einsum("sp,dp->sd", tail_dz, proj_part, preferred_element_type=jnp.float32)
    tail_loss = jnp.where(member, log_total - target_logit, 0.0)
    return (out_grad, proj_grad, returned, tail_loss)


def on_device(
    hidden,
    pre_gates,
    conv_weight,
    head_weight,
    cluster_weight,
    tail1_proj,
    tail2_proj,
    tail1_out,
    tail2_out,
    cluster_id,
    target,
):
    tokens = hidden.shape[0]
    model_width = hidden.shape[1]
    owners = lax.axis_size("tok")
    groups = lax.axis_size("ch")
    ch_index = lax.axis_index("ch")
    capacity = max(2, tokens // owners)
    narrow = model_width // groups
    col_start = ch_index * narrow
    sentinel = owners * capacity
    is_tail = cluster_id >= 0
    owner_ids = jnp.where(is_tail, cluster_id // 2, 0)
    tier_ids = jnp.where(is_tail, cluster_id % 2, -1)
    owner_range = jnp.arange(owners, dtype=jnp.int32)
    owner_hits = ((owner_ids[:, None] == owner_range[None, :]) & is_tail[:, None]).astype(jnp.int32)
    running = jnp.cumsum(owner_hits, axis=0)
    slot_ids = jnp.sum(running * owner_hits, axis=1) - 1
    flat_index = jnp.where(is_tail, owner_ids * capacity + slot_ids, sentinel)
    send_rows = (
        jnp.zeros((sentinel + 1, hidden.shape[1]), jnp.bfloat16)
        .at[flat_index]
        .set(hidden)[:sentinel]
    )
    send_meta = (
        jnp.full((sentinel + 1, 2), -1, jnp.int32)
        .at[flat_index]
        .set(jnp.stack([target, tier_ids], axis=1))[:sentinel]
    )
    got_rows, got_meta = (
        lax.all_to_all(
            send_rows.reshape(owners, capacity, -1), "tok", split_axis=0, concat_axis=0, tiled=True
        ),
        lax.all_to_all(
            send_meta.reshape(owners, capacity, 2), "tok", split_axis=0, concat_axis=0, tiled=True
        ),
    )
    conv_full, head_full, cluster_full = (
        lax.all_gather(conv_weight, "tok", axis=2, tiled=True),
        lax.all_gather(head_weight, "tok", axis=0, tiled=True),
        lax.all_gather(cluster_weight, "tok", axis=0, tiled=True),
    )
    word_logits = jnp.dot(hidden, head_full, preferred_element_type=jnp.float32)
    cluster_logits = jnp.dot(hidden, cluster_full, preferred_element_type=jnp.float32)
    head_max = jnp.maximum(jnp.max(word_logits, axis=1), jnp.max(cluster_logits, axis=1))
    word_terms = jnp.exp(word_logits - head_max[:, None])
    cluster_terms = jnp.exp(cluster_logits - head_max[:, None])
    head_sum = jnp.sum(word_terms, axis=1) + jnp.sum(cluster_terms, axis=1)
    head_value = jnp.dot(
        word_terms.astype(jnp.bfloat16), head_full.T, preferred_element_type=jnp.float32
    )
    head_value = head_value + jnp.dot(
        cluster_terms.astype(jnp.bfloat16), cluster_full.T, preferred_element_type=jnp.float32
    )
    head_words = head_full.shape[1]
    cluster_cols = cluster_full.shape[1]
    word_local = target - ch_index * head_words
    in_words = ~is_tail & (word_local >= 0) & (word_local < head_words)
    word_column = jnp.clip(word_local, 0, head_words - 1)
    cluster_local = cluster_id - ch_index * cluster_cols
    in_clusters = is_tail & (cluster_local >= 0) & (cluster_local < cluster_cols)
    cluster_column = jnp.clip(cluster_local, 0, cluster_cols - 1)
    word_pick = jnp.take_along_axis(word_logits, word_column[:, None], axis=1)[:, 0]
    cluster_pick = jnp.take_along_axis(cluster_logits, cluster_column[:, None], axis=1)[:, 0]
    head_target = jnp.where(in_words, word_pick, 0.0) + jnp.where(in_clusters, cluster_pick, 0.0)
    word_vector = jnp.take(head_full, word_column, axis=1).T.astype(jnp.float32)
    cluster_vector = jnp.take(cluster_full, cluster_column, axis=1).T.astype(jnp.float32)
    target_vector = jnp.where(in_words[:, None], word_vector, 0.0) + jnp.where(
        in_clusters[:, None], cluster_vector, 0.0
    )
    rows_in = got_rows.reshape(sentinel, -1)
    word_ids = got_meta[:, :, 0].reshape(sentinel)
    tiers = got_meta[:, :, 1].reshape(sentinel)
    first_member = tiers == 0
    second_member = tiers == 1
    first_proj = tail1_proj[0]
    second_proj = tail2_proj[0]
    first_part = lax.dynamic_slice_in_dim(first_proj, col_start, narrow, 0)
    second_part = lax.dynamic_slice_in_dim(second_proj, col_start, narrow, 0)
    rows_part = lax.dynamic_slice_in_dim(rows_in, col_start, narrow, 1)
    first_z = jnp.dot(rows_in, first_proj, preferred_element_type=jnp.float32)
    second_z = jnp.dot(rows_in, second_proj, preferred_element_type=jnp.float32)
    first_features = first_z.astype(jnp.bfloat16)
    second_features = second_z.astype(jnp.bfloat16)
    first_logits, first_inside, first_column, first_totals = tier_local(
        first_features, word_ids, first_member, tail1_out[0], ch_index
    )
    second_logits, second_inside, second_column, second_totals = tier_local(
        second_features, word_ids, second_member, tail2_out[0], ch_index
    )
    head_totals, first_totals, second_totals = merged(
        ((head_max, head_sum, head_value, target_vector, head_target), first_totals, second_totals),
        "ch",
        joined_all,
    )
    merged_max, merged_sum, merged_value, merged_vector, merged_target = head_totals
    full_grad = merged_value / merged_sum[:, None] - merged_vector
    head_grad = lax.dynamic_slice_in_dim(full_grad, col_start, narrow, 1)
    first_out_grad, first_proj_grad, first_back, first_loss = tier_finish(
        first_features,
        first_logits,
        first_inside,
        first_column,
        first_member,
        first_totals,
        rows_part,
        first_part,
    )
    second_out_grad, second_proj_grad, second_back, second_loss = tier_finish(
        second_features,
        second_logits,
        second_inside,
        second_column,
        second_member,
        second_totals,
        rows_part,
        second_part,
    )
    tail_back = first_back + second_back
    tail_loss = first_loss + second_loss
    back_rows, back_loss = (
        lax.all_to_all(
            tail_back.reshape(owners, capacity, narrow).astype(jnp.bfloat16),
            "tok",
            split_axis=0,
            concat_axis=0,
            tiled=True,
        ).astype(jnp.float32),
        lax.all_to_all(
            tail_loss.reshape(owners, capacity).astype(jnp.bfloat16),
            "tok",
            split_axis=0,
            concat_axis=0,
            tiled=True,
        ).astype(jnp.float32),
    )
    back_flat = jnp.concatenate(
        [back_rows.reshape(sentinel, narrow), jnp.zeros((1, narrow), jnp.float32)], axis=0
    )
    loss_flat = jnp.concatenate([back_loss.reshape(sentinel), jnp.zeros((1,), jnp.float32)], axis=0)
    token_loss = merged_max + jnp.log(merged_sum) - merged_target + loss_flat[flat_index]
    grad_sum = head_grad + back_flat[flat_index]
    gate_a = pre_gates[0].astype(jnp.float32)
    gate_sig = jax.nn.sigmoid(pre_gates[1].astype(jnp.float32))
    gate_grads = jnp.stack(
        [grad_sum * gate_sig, grad_sum * gate_a * gate_sig * (1.0 - gate_sig)]
    ).astype(jnp.bfloat16)
    blocks = gate_grads.reshape(2, tokens // LEN, LEN, narrow)
    shifted = jnp.stack(
        [
            jnp.pad(blocks[:, :, offset_rows:], ((0, 0), (0, 0), (0, offset_rows), (0, 0))).reshape(
                2, tokens, narrow
            )
            for offset_rows in range(K)
        ]
    )
    conv_terms = jnp.einsum("kgtc,gkrc->tr", shifted, conv_full, preferred_element_type=jnp.float32)
    conv_grad = lax.psum_scatter(
        conv_terms.astype(jnp.bfloat16), "ch", scatter_dimension=1, tiled=True
    ).astype(jnp.float32)
    grad_input = (grad_sum + conv_grad).astype(jnp.bfloat16)
    return (
        token_loss,
        grad_input,
        first_proj_grad[None],
        second_proj_grad[None],
        first_out_grad[None],
        second_out_grad[None],
    )


def solution(mesh):
    placed = (
        P("tok", None),
        P(None, "tok", "ch"),
        P(None, None, "tok", "ch"),
        P("tok", "ch"),
        P("tok", "ch"),
        P("tok", None, None),
        P("tok", None, None),
        P("tok", None, "ch"),
        P("tok", None, "ch"),
        P("tok"),
        P("tok"),
    )
    return jax.shard_map(
        on_device,
        mesh=mesh,
        in_specs=placed,
        out_specs=(
            P("tok"),
            P("tok", "ch"),
            P("tok", "ch", None),
            P("tok", "ch", None),
            P("tok", None, "ch"),
            P("tok", None, "ch"),
        ),
        check_vma=False,
    )
```

profile of v0, /device:TPU:0, one launch (start us, length us, event | category | flops | bytes accessed | tf_op | source)
XLA Modules:
  0.0 462.4 jit_solution(16528666124955097297)
XLA Ops:
  12.9 8.3 %all-to-all-start = ((s32[16,8,2]{1,2,0:T(2,128)}), s32[16,8,2]{1,2,0:T(2,128)S(1)}, u32[]{:S(2)}, u32[]{:S(2)}) async-start(s32[16,8,2]{1,2,0:T(2,128)} %copy.86), calls=%async_computation | async-start | bytes 32768 | tf_op jit(solution)/shard_map/all_to_all | solution.py:125
  21.2 42.5 %all-gather.13 = bf16[16,64,16]{1,2,0:T(8,128)(2,1)S(1)} all-gather(bf16[1,64,16]{1,2,0:T(8,128)(2,1)} %bitcast.371), channel_id=1, replica_groups=mesh['tok'=16,'ch'=2] {'tok'}, dimensions={0}, use_global_device_ids=true | all-gather | bytes 34816 | tf_op jit(solution)/shard_map/all_gather | solution.py:132
  68.4 177.2 %all-gather.28.cloned.1.call-done = bf16[1024,10240]{1,0:T(8,128)(2,1)} async-done(((bf16[64,10240]{1,0:T(8,128)(2,1)}), bf16[1024,10240]{1,0:T(8,128)(2,1)}) %all-gather.28.cloned.1.call-update) | async-done | bytes 20971536 | tf_op jit(solution)/shard_map/all_gather | solution.py:131
  245.6 12.3 %fusion.155 = (f32[128]{0:T(128)S(1)}, f32[128,10240]{1,0:T(8,128)}) fusion(bf16[128,1024]{1,0:T(8,128)(2,1)S(1)} %copy-done.10, bf16[1024,10240]{1,0:T(8,128)(2,1)} %all-gather.28.cloned.1.call-done), kind=kOutput, calls=%fused_computation.289 | convolution fusion | flops 2685665280 | bytes 26477056 | tf_op jit(solution)/shard_map/dot_general | solution.py:134
  257.9 2.1 gather_fusion.6
  260.6 28.0 %copy.112 = bf16[1024,10240]{0,1:T(8,128)(2,1)} copy(bf16[1024,10240]{1,0:T(8,128)(2,1)} %all-gather.28.cloned.1.call-done) | data formatting | bytes 41943040 | tf_op jit(solution)/shard_map/all_gather | solution.py:131
  288.6 10.7 %gather_fusion.1 = bf16[128,1024]{1,0:T(8,128)(2,1)S(1)} fusion(bf16[1024,10240]{0,1:T(8,128)(2,1)} %copy.112, s32[1024]{0:T(1024)S(1)} %pad_clamp_fusion.3), kind=kCustom, calls=%fused_computation.1 | custom fusion | bytes 524800 | tf_op jit(solution)/shard_map/jit(_take)/gather | solution.py:157
  300.7 13.0 %fusion.2 = f32[128,1024]{1,0:T(8,128)S(1)} fusion(bf16[1024,10240]{1,0:T(8,128)(2,1)} %all-gather.28.cloned.1.call-done, f32[128,10240]{1,0:T(8,128)} %get-tuple-element.163, f32[128]{0:T(128)S(1)} %max.95), kind=kOutput, calls=%fused_computation.17 | convolution fusion | flops 2686976000 | bytes 26739200 | tf_op jit(solution)/shard_map/dot_general | solution.py:140
  317.3 3.6 all-to-all-start.1
  325.5 2.1 gather_fusion.4
  332.7 2.1 all-gather.10
  340.7 2.9 fusion.154
  343.6 2.8 gather_fusion.8
  377.0 6.9 %all-to-all-start.2 = ((bf16[16,1,8]{2,1,0:T(2,128)(2,1)}), bf16[16,1,8]{2,1,0:T(2,128)(2,1)}, u32[]{:S(2)}, u32[]{:S(2)}) async-start(bf16[16,1,8]{2,1,0:T(2,128)(2,1)} %copy.111), calls=%async_computation.2 | async-start | bytes 16384 | tf_op jit(solution)/shard_map/all_to_all | solution.py:220
  387.8 2.0 all-gather.9
  391.5 6.9 %all-to-all-start.3 = ((bf16[16,8,512]{2,1,0:T(8,128)(2,1)}), bf16[16,8,512]{2,1,0:T(8,128)(2,1)S(1)}, u32[]{:S(2)}, u32[]{:S(2)}) async-start(bf16[16,8,512]{2,1,0:T(8,128)(2,1)} %fusion.18), calls=%async_computation.3 | async-start | bytes 262144 | tf_op jit(solution)/shard_map/all_to_all | solution.py:213
  398.4 2.2 convolution_bitcast_fusion.2
  402.9 6.5 %all-to-all-done.3 = bf16[16,8,512]{2,1,0:T(8,128)(2,1)S(1)} async-done(((bf16[16,8,512]{2,1,0:T(8,128)(2,1)}), bf16[16,8,512]{2,1,0:T(8,128)(2,1)S(1)}, u32[]{:S(2)}, u32[]{:S(2)}) %all-to-all-start.3) | async-done | bytes 131104 | tf_op jit(solution)/shard_map/all_to_all | solution.py:213
  414.6 3.4 fusion.1
  422.0 2.3 fusion.151
  430.1 9.8 %all-gather.30.cloned.1.call-done = bf16[2,4,1024,512]{3,2,1,0:T(8,128)(2,1)} async-done(((bf16[2,4,64,512]{3,2,1,0:T(8,128)(2,1)}), bf16[2,4,1024,512]{3,2,1,0:T(8,128)(2,1)}) %all-gather.30.cloned.1.call-update) | async-done | bytes 8388624 | tf_op jit(solution)/shard_map/all_gather | solution.py:130
  440.0 7.2 %fusion.8 = bf16[128,1024]{1,0:T(8,128)(2,1)} fusion(bf16[2,4,1024,512]{3,2,1,0:T(8,128)(2,1)} %all-gather.30.cloned.1.call-done, bf16[1,2,128,512]{3,2,1,0:T(8,128)(2,1)} %pad_bitcast_fusion, bf16[1,2,128,512]{3,2,1,0:T(8,128)(2,1)} %pad_bitcast_fusion.1, bf16[1,2,128,512]{3,2,1,0:T(8,128)(2,1)} %pad_bitcast_fusion.2, ...), kind=kOutput, calls=%fused_computation.28 | convolution fusion | flops 1075970048 | bytes 9699328 | tf_op jit(solution)/shard_map/kgtc,gkrc->tr/dot_general | solution.py:248
  448.9 2.8 convolution_bitcast_fusion.1
  451.7 2.0 convolution_bitcast_fusion
  (271 shorter events, 87.9 us)
Async XLA Ops:
  7.2 332.4 %copy-start = (bf16[1,1024,256]{2,1,0:T(8,128)(2,1)S(1)}, bf16[1,1024,256]{2,1,0:T(8,128)(2,1)}, u32[]{:S(2)}) copy-start(bf16[1,1024,256]{2,1,0:T(8,128)(2,1)} %param.16) | copy-start | bytes 1572868
  7.2 238.4 %all-gather.28.cloned.1.call-start = ((), (), s32[]{:S(2)}) async-start(), calls=%async_computation.5 | async-start | bytes 22282240 | tf_op jit(solution)/shard_map/all_gather | solution.py:131
  7.9 237.7 %copy-start.10 = (bf16[128,1024]{1,0:T(8,128)(2,1)S(1)}, bf16[128,1024]{1,0:T(8,128)(2,1)}, u32[]{:S(2)}) copy-start(bf16[128,1024]{1,0:T(8,128)(2,1)} %param.11) | copy-start | bytes 786436
  12.9 53.8 %all-to-all-start = ((s32[16,8,2]{1,2,0:T(2,128)}), s32[16,8,2]{1,2,0:T(2,128)S(1)}, u32[]{:S(2)}, u32[]{:S(2)}) async-start(s32[16,8,2]{1,2,0:T(2,128)} %copy.86), calls=%async_computation | async-start | bytes 32768 | tf_op jit(solution)/shard_map/all_to_all | solution.py:125
  21.2 400.9 %all-gather.34.cloned.1.call-start = ((), (), s32[]{:S(2)}) async-start(), calls=%async_computation.9 | async-start | bytes 1572864 | tf_op jit(solution)/shard_map/all_gather | solution.py:11
  68.4 191.6 %copy-start.30 = (s32[128]{0:T(128)S(1)}, s32[128]{0:T(128)}, u32[]{:S(2)}) copy-start(s32[128]{0:T(128)} %param.20) | copy-start | bytes 1540
  68.4 191.6 %copy-start.31 = (s32[128]{0:T(128)S(1)}, s32[128]{0:T(128)}, u32[]{:S(2)}) copy-start(s32[128]{0:T(128)} %param.21) | copy-start | bytes 1540
  300.4 123.9 %all-gather.32.cloned.1.call-start = ((), (), s32[]{:S(2)}) async-start(), calls=%async_computation.8 | async-start | bytes 1572864 | tf_op jit(solution)/shard_map/all_gather | solution.py:11
  300.6 13.1 %copy-start.21 = (f32[128]{0:T(128)}, f32[128]{0:T(128)S(1)}, u32[]{:S(2)}) copy-start(f32[128]{0:T(128)S(1)} %max.95) | copy-start | bytes 1540
  313.7 8.6 %copy-start.3 = (bf16[1,256,1536]{2,1,0:T(8,128)(2,1)S(1)}, bf16[1,256,1536]{2,1,0:T(8,128)(2,1)}, u32[]{:S(2)}) copy-start(bf16[1,256,1536]{2,1,0:T(8,128)(2,1)} %param.18) | copy-start | bytes 2359300
  314.8 125.1 %all-gather.30.cloned.1.call-start = ((), (), s32[]{:S(2)}) async-start(), calls=%async_computation.6 | async-start | bytes 8912896 | tf_op jit(solution)/shard_map/all_gather | solution.py:130
  317.3 17.5 %all-to-all-start.1 = ((bf16[16,8,1024]{2,1,0:T(8,128)(2,1)}), bf16[16,8,1024]{2,1,0:T(8,128)(2,1)S(1)}, u32[]{:S(2)}, u32[]{:S(2)}) async-start(bf16[16,8,1024]{2,1,0:T(8,128)(2,1)} %slice_bitcast_fusion), calls=%async_computation.1 | async-start | bytes 524288 | tf_op jit(solution)/shard_map/all_to_all | solution.py:122
  320.9 14.7 %copy-start.13 = (bf16[1,1024,64]{1,2,0:T(8,128)(2,1)S(1)}, bf16[1,1024,64]{1,2,0:T(8,128)(2,1)}, u32[]{:S(2)}) copy-start(bf16[1,1024,64]{1,2,0:T(8,128)(2,1)} %param.17) | copy-start | bytes 393220
  323.4 11.4 %copy-start.48 = (s32[128]{0:T(128)}, s32[128]{0:T(128)S(1)}, u32[]{:S(2)}) copy-start(s32[128]{0:T(128)S(1)} %min.64) | copy-start | bytes 1540
  377.0 14.5 %all-to-all-start.2 = ((bf16[16,1,8]{2,1,0:T(2,128)(2,1)}), bf16[16,1,8]{2,1,0:T(2,128)(2,1)}, u32[]{:S(2)}, u32[]{:S(2)}) async-start(bf16[16,1,8]{2,1,0:T(2,128)(2,1)} %copy.111), calls=%async_computation.2 | async-start | bytes 16384 | tf_op jit(solution)/shard_map/all_to_all | solution.py:220
  385.4 13.0 %copy-start.7 = (bf16[16,8,1024]{2,1,0:T(8,128)(2,1)S(1)}, bf16[16,8,1024]{2,1,0:T(8,128)(2,1)}, u32[]{:S(2)}) copy-start(bf16[16,8,1024]{2,1,0:T(8,128)(2,1)} %copy-done.6) | copy-start | bytes 786436
  385.4 13.0 %copy-start.36 = (pred[128]{0:T(512)(128)(4,1)S(1)}, pred[128]{0:T(512)(128)(4,1)}, u32[]{:S(2)}) copy-start(pred[128]{0:T(512)(128)(4,1)} %copy-done.34) | copy-start | bytes 388
  391.5 21.1 %copy-start.52 = (f32[1,1,128]{2,1,0:T(1,128)S(1)}, f32[1,1,128]{2,1,0:T(1,128)}, u32[]{:S(2)}) copy-start(f32[1,1,128]{2,1,0:T(1,128)} %get-tuple-element.128) | copy-start | bytes 1540
  391.5 23.1 %copy-start.22 = (f32[128]{0:T(128)S(1)}, f32[128]{0:T(128)}, u32[]{:S(2)}) copy-start(f32[128]{0:T(128)} %copy-done.21) | copy-start | bytes 1540
  391.5 18.0 %all-to-all-start.3 = ((bf16[16,8,512]{2,1,0:T(8,128)(2,1)}), bf16[16,8,512]{2,1,0:T(8,128)(2,1)S(1)}, u32[]{:S(2)}, u32[]{:S(2)}) async-start(bf16[16,8,512]{2,1,0:T(8,128)(2,1)} %fusion.18), calls=%async_computation.3 | async-start | bytes 262144 | tf_op jit(solution)/shard_map/all_to_all | solution.py:213
  398.4 55.9 %reduce-scatter.2.cloned.1.call-start = ((), (), s32[]{:S(2)}) async-start(), calls=%async_computation.7 | async-start | bytes 393216 | tf_op jit(solution)/shard_map/reduce_scatter | solution.py:249
  430.1 17.1 %copy-start.27 = (pred[128]{0:T(512)(128)(4,1)S(1)}, pred[128]{0:T(512)(128)(4,1)}, u32[]{:S(2)}) copy-start(pred[128]{0:T(512)(128)(4,1)} %copy-done.25) | copy-start | bytes 388
  430.1 18.7 %copy-start.33 = (pred[128]{0:T(512)(128)(4,1)S(1)}, pred[128]{0:T(512)(128)(4,1)}, u32[]{:S(2)}) copy-start(pred[128]{0:T(512)(128)(4,1)} %copy-done.32) | copy-start | bytes 388
  430.1 18.7 %copy-start.49 = (s32[128]{0:T(128)S(1)}, s32[128]{0:T(128)}, u32[]{:S(2)}) copy-start(s32[128]{0:T(128)} %copy-done.48) | copy-start | bytes 1540
  (38 other events, 146.8 us)
Sparse Core Ops, SparseCore 0:
  10.8 234.7 all-gather.27
  300.5 7.2 all-gather.33
  314.9 6.9 all-gather.31
  324.6 115.3 all-gather.29
  447.4 6.8 reduce-scatter.1
where the time goes:
time: 464 us; the launch traced here: 462 us
  waiting for transfers between devices  195 us (42%)
  local copies, waits for them, and re-layouts  88.4 us (19%)
  blocking collectives  66.9 us (14%)
  matrix products  51.7 us (11%)
  starting transfers between devices  26.1 us (6%)
  other arithmetic  19.2 us (4%)
  between operations  14.7 us (3%)
    all_gather x1, waiting for transfers between devices, on_device(): lax.all_gather(head_weight, 'tok', axis=0, tiled=True)  177 us
    all_gather x1, blocking collectives, on_device(): lax.all_gather(cluster_weight, 'tok', axis=0, tiled=True)  42.5 us
    all_gather x1, local copies, waits for them, and re-layouts, on_device(): lax.all_gather(head_weight, 'tok', axis=0, tiled=True)  28 us
    all_gather x13, blocking collectives, merged(): everything = jax.tree.map(lambda part: lax.all_gather(part, axis), x)  24.4 us
    dot_general x1, matrix products, on_device(): jnp.dot(word_terms.astype(jnp.bfloat16), head_full.T, preferred_element_t...  13 us
    dot_general x1, matrix products, on_device(): word_logits = jnp.dot(hidden, head_full, preferred_element_type=jnp.float32)  12.3 us
    gather x1, local copies, waits for them, and re-layouts, on_device(): word_vector = jnp.take(head_full, word_column, axis=1).T.astype(jnp.float32)  10.7 us
    all_gather x1, waiting for transfers between devices, on_device(): lax.all_gather(conv_weight, 'tok', axis=2, tiled=True)  9.81 us
  transfers between devices with their start and end apart: 9, of which 4 were waited for; matrix products, arithmetic and copies ran while one was open for 20% of the time, Pallas kernels for 0%

commit v1 on v0

v1 whole, which is shorter than its diff:
```python
import jax
import jax.numpy as jnp
from jax import lax
from jax.sharding import Mesh, PartitionSpec as P

K = 4
LEN = 128
LANES = 128
TOK = ("hi", "lo")
BF = jnp.bfloat16
F32 = jnp.float32


def dot(a, b):
    return jnp.dot(a, b, preferred_element_type=F32)


def dot_t(a, b):
    return lax.dot_general(a, b, (((1,), (1,)), ((), ())), preferred_element_type=F32)


def t_dot(a, b):
    return lax.dot_general(a, b, (((0,), (0,)), ((), ())), preferred_element_type=F32)


def merge_stats(stats):
    top = jnp.max(stats[:, 0], axis=0)
    total = jnp.sum(stats[:, 1] * jnp.exp(stats[:, 0] - top), axis=0)
    return top, total


def running_count(mine):
    local = mine.shape[1]
    upto = (jnp.arange(local)[:, None] <= jnp.arange(local)[None, :]).astype(F32)
    within = dot(mine, upto)
    blocks = mine.shape[0]
    before = (jnp.arange(blocks)[None, :] < jnp.arange(blocks)[:, None]).astype(F32)
    return within + dot(before, within[:, -1:])


def tier_start(rows, word_ids, proj, out_shard, ch_index):
    features = dot(rows, proj).astype(BF)
    logits = dot(features, out_shard)
    top = jnp.max(logits, axis=1)
    total = jnp.sum(jnp.exp(logits - top[:, None]), axis=1)
    width = out_shard.shape[1]
    positions = jnp.arange(width, dtype=jnp.int32) + ch_index * width
    hot = positions[None, :] == word_ids[:, None]
    picked = jnp.sum(jnp.where(hot, logits, 0.0), axis=1)
    return features, logits, hot, picked, jnp.stack([top, total])


def tier_slope(logits, hot, member, log_total):
    slope = jnp.exp(logits - log_total[:, None]) - hot.astype(F32)
    return jnp.where(member[:, None], slope, 0.0).astype(BF)


def on_device(
    hidden,
    pre_gates,
    conv_weight,
    head_weight,
    cluster_weight,
    tail1_proj,
    tail2_proj,
    tail1_out,
    tail2_out,
    cluster_id,
    target,
):
    local, model_width = hidden.shape
    owners = lax.axis_size(TOK)
    groups = lax.axis_size("ch")
    lo = lax.axis_size("lo")
    me = lax.axis_index(TOK)
    ch_index = lax.axis_index("ch")
    tokens = local * owners
    slots = max(2, local // owners) * owners
    narrow = model_width // groups
    col_start = ch_index * narrow

    hidden_part = lax.dynamic_slice_in_dim(hidden, col_start, narrow, 1)
    hidden_cols = lax.all_gather(hidden_part, TOK, axis=0, tiled=True)
    hidden_all = lax.all_gather(hidden_cols, "ch", axis=1, tiled=True)
    meta = lax.all_gather(jnp.stack([cluster_id, target]), TOK, axis=1, tiled=True)
    cluster_all, target_all = meta[0], meta[1]

    words = head_weight.shape[1] // owners
    clusters = cluster_weight.shape[1]
    word_part = lax.all_to_all(head_weight, TOK, split_axis=1, concat_axis=0, tiled=True)
    cluster_part = lax.all_gather(cluster_weight, TOK, axis=0, tiled=True)
    conv_part = lax.all_gather(conv_weight, "hi", axis=2, tiled=True)

    mine = (cluster_all >= 0) & (cluster_all // 2 == me)
    rank = running_count(mine.reshape(owners, local).astype(F32)).reshape(tokens)
    slot_ids = jnp.where(mine, rank.astype(jnp.int32) - 1, -1)
    chosen = slot_ids[:, None] == jnp.arange(slots, dtype=jnp.int32)[None, :]
    chosen_bf = chosen.astype(BF)
    rows = t_dot(chosen_bf, hidden_all).astype(BF)
    word_ids = jnp.sum(jnp.where(chosen, target_all[:, None], 0), axis=0)
    tiers = jnp.sum(jnp.where(chosen, cluster_all[:, None] % 2 + 1, 0), axis=0)
    first_member, second_member = tiers == 1, tiers == 2
    first_proj, second_proj = tail1_proj[0], tail2_proj[0]
    first_out, second_out = tail1_out[0], tail2_out[0]
    first_features, first_logits, first_hot, first_pick, first_stats = tier_start(
        rows, word_ids, first_proj, first_out, ch_index
    )
    second_features, second_logits, second_hot, second_pick, second_stats = tier_start(
        rows, word_ids, second_proj, second_out, ch_index
    )
    stats = lax.all_gather(jnp.stack([first_stats, second_stats], axis=1), "ch")
    top, total = merge_stats(stats)
    tail_log = top + jnp.log(total)
    first_slope = tier_slope(first_logits, first_hot, first_member, tail_log[0])
    second_slope = tier_slope(second_logits, second_hot, second_member, tail_log[1])
    dz = jnp.concatenate(
        [dot_t(first_slope, first_out), dot_t(second_slope, second_out)], axis=1
    )
    dz = jnp.sum(lax.all_gather(dz, "ch"), axis=0).astype(BF)
    first_dz = dz[:, : first_proj.shape[1]]
    second_dz = dz[:, first_proj.shape[1] :]
    back = dot_t(first_dz, first_proj) + dot_t(second_dz, second_proj)
    col_group = jnp.arange(model_width, dtype=jnp.int32)[None, :] // narrow
    back = jnp.where(col_group == ch_index, back, 0.0).astype(BF)
    once = jnp.where(ch_index == 0, 1.0, 0.0)
    tail_loss = jnp.where(first_member, once * tail_log[0] - first_pick, 0.0)
    tail_loss = tail_loss + jnp.where(second_member, once * tail_log[1] - second_pick, 0.0)
    first_out_grad = t_dot(first_features, first_slope)
    second_out_grad = t_dot(second_features, second_slope)
    rows_part = lax.dynamic_slice_in_dim(rows, col_start, narrow, 1)
    first_proj_grad = t_dot(rows_part, first_dz)
    second_proj_grad = t_dot(rows_part, second_dz)

    spare = -(words + clusters) % LANES
    columns = jnp.concatenate(
        [word_part, cluster_part, jnp.zeros((model_width, spare), BF)], axis=1
    )
    place = jnp.arange(columns.shape[1], dtype=jnp.int32)[None, :]
    limit = jnp.where(me == 0, words + clusters, words)
    logits = jnp.where(place < limit, dot(hidden_all, columns), -jnp.inf)
    top = jnp.max(logits, axis=1)
    total = jnp.sum(jnp.exp(logits - top[:, None]), axis=1)
    is_tail = cluster_all >= 0
    word_place = target_all - (ch_index * owners + me) * words
    word_place = jnp.where((word_place >= 0) & (word_place < words), word_place, -1)
    cluster_place = cluster_all - ch_index * clusters
    cluster_here = (cluster_place >= 0) & (cluster_place < clusters) & (me == 0)
    cluster_place = jnp.where(cluster_here, cluster_place + words, -1)
    hot = place == jnp.where(is_tail, cluster_place, word_place)[:, None]
    picked = jnp.sum(jnp.where(hot, logits, 0.0), axis=1)
    stats = lax.all_gather(jnp.stack([top, total]), "ch")
    stats = lax.all_gather(jnp.stack(merge_stats(stats)), TOK)
    top, total = merge_stats(stats)
    head_log = top + jnp.log(total)
    slope = (jnp.exp(logits - head_log[:, None]) - hot.astype(F32)).astype(BF)
    grad_part = dot_t(
        jnp.concatenate([slope, chosen_bf], axis=1),
        jnp.concatenate([columns, back.T], axis=1),
    ).astype(BF)
    grad_cols = lax.psum_scatter(grad_part, "ch", scatter_dimension=1, tiled=True)
    grad_sum = lax.psum_scatter(grad_cols, TOK, scatter_dimension=0, tiled=True).astype(F32)

    loss_part = jnp.sum(jnp.where(chosen, tail_loss[None, :], 0.0), axis=1) - picked
    loss_part = jnp.sum(lax.all_gather(loss_part, "ch"), axis=0)
    own_loss = lax.psum_scatter(loss_part, TOK, scatter_dimension=0, tiled=True)
    token_loss = own_loss + lax.dynamic_slice_in_dim(head_log, me * local, local, 0)

    gate_a = pre_gates[0].astype(F32)
    gate_sig = jax.nn.sigmoid(pre_gates[1].astype(F32))
    gate_grads = jnp.stack(
        [grad_sum * gate_sig, grad_sum * gate_a * gate_sig * (1.0 - gate_sig)]
    ).astype(BF)
    gates = lax.all_gather(gate_grads, "lo", axis=1, tiled=True)
    near = gates.shape[1]
    blocks = gates.reshape(2, near // LEN, LEN, narrow)
    shifted = jnp.stack(
        [
            jnp.pad(blocks[:, :, offset:], ((0, 0), (0, 0), (0, offset), (0, 0))).reshape(
                2, near, narrow
            )
            for offset in range(K)
        ]
    )
    conv_terms = jnp.einsum(
        "kgtc,gkrc->tr", shifted, conv_part, preferred_element_type=F32
    ).astype(BF)
    conv_terms = lax.all_to_all(
        conv_terms.reshape(lo, local, -1), "lo", split_axis=0, concat_axis=0, tiled=True
    )
    share = conv_weight.shape[2]
    conv_terms = conv_terms.reshape(lo, local, -1, share).transpose(1, 2, 0, 3)
    conv_grad = lax.psum_scatter(
        conv_terms.reshape(local, model_width), "ch", scatter_dimension=1, tiled=True
    )
    grad_input = (grad_sum + conv_grad.astype(F32)).astype(BF)
    return (
        token_loss,
        grad_input,
        first_proj_grad[None],
        second_proj_grad[None],
        first_out_grad[None],
        second_out_grad[None],
    )


def solution(mesh):
    n_tok, n_ch = mesh.shape["tok"], mesh.shape["ch"]
    lo = 1
    while n_tok % (lo * 2) == 0 and lo * lo * 4 <= n_tok:
        lo *= 2
    split = Mesh(mesh.devices.reshape(n_tok // lo, lo, n_ch), ("hi", "lo", "ch"))
    placed = (
        P(TOK, None),
        P(None, TOK, "ch"),
        P(None, None, TOK, "ch"),
        P(TOK, "ch"),
        P(TOK, "ch"),
        P(TOK, None, None),
        P(TOK, None, None),
        P(TOK, None, "ch"),
        P(TOK, None, "ch"),
        P(TOK),
        P(TOK),
    )
    return jax.shard_map(
        on_device,
        mesh=split,
        in_specs=placed,
        out_specs=(
            P(TOK),
            P(TOK, "ch"),
            P(TOK, "ch", None),
            P(TOK, "ch", None),
            P(TOK, None, "ch"),
            P(TOK, None, "ch"),
        ),
        check_vma=False,
    )
```

time: 464 us -> 489 us (1.054)
  blocking collectives: 66.9 us -> 179 us
  local copies, waits for them, and re-layouts: 88.4 us -> 14.2 us
  waiting for transfers between devices: 195 us -> 224 us
  matrix products: 51.7 us -> 31.9 us
  starting transfers between devices: 26.1 us -> 8.29 us
    reduce_scatter x1 -> x3, waiting for transfers between devices: 0.51 us -> 94 us  [the longest x1 84 us: on_device(): lax.psum_scatter(grad_cols, TOK, scatter_dimension=0, tiled=True)]
    all_gather x14 -> x7, blocking collectives: 66.9 us -> 138 us  [the longest x1 55.3 us: on_device(): cluster_part = lax.all_gather(cluster_weight, TOK, axis=0, tiled=True)]
    all_gather x4, waiting for transfers between devices: 187 us -> 129 us  [the longest x1 65.8 us: on_device(): hidden_cols = lax.all_gather(hidden_part, TOK, axis=0, tiled=True)]
    unnamed x0 -> x1, blocking collectives: none -> 41.1 us
    all_gather x2 -> x1, local copies, waits for them, and re-layouts: 28 us -> 0.01 us  [on_device(): loss_part = jnp.sum(lax.all_gather(loss_part, 'ch'), axis=0)]
    gather x11 -> x0, local copies, waits for them, and re-layouts: 25.7 us -> none  [the longest x1 10.7 us: on_device(): word_vector = jnp.take(head_full, word_column, axis=1).T.astype(jnp.float32)]
    dot_general x17 -> x18, matrix products: 51.7 us -> 31.9 us  [the longest x5 9.85 us: dot_t(): lax.dot_general(a, b, (((1,), (1,)), ((), ())), preferred_element_type=F32)]
    all_to_all x4 -> x2, starting transfers between devices: 25.7 us -> 8.05 us  [the longest x1 4.38 us: on_device(): lax.all_to_all(head_weight, TOK, split_axis=1, concat_axis=0, tiled=True)]
  transfers between devices with their start and end apart: 9 -> 9, of which waited for: 4 -> 5; matrix products, arithmetic and copies ran while one was open for 20% -> 6% of each run, Pallas kernels for 0% -> 0%
where the time goes in v1:
time: 489 us; the launch traced here: 488 us
  waiting for transfers between devices  224 us (46%)
  blocking collectives  179 us (37%)
  matrix products  31.9 us (7%)
  other arithmetic  15.6 us (3%)
  between operations  15.4 us (3%)
  local copies, waits for them, and re-layouts  14.2 us (3%)
  starting transfers between devices  8.29 us (2%)
    reduce_scatter x1, waiting for transfers between devices, on_device(): lax.psum_scatter(grad_cols, TOK, scatter_dimension=0, tiled=True)  84 us
    all_gather x1, waiting for transfers between devices, on_device(): hidden_cols = lax.all_gather(hidden_part, TOK, axis=0, tiled=True)  65.8 us
    all_gather x1, blocking collectives, on_device(): cluster_part = lax.all_gather(cluster_weight, TOK, axis=0, tiled=True)  55.3 us
    unnamed x1, blocking collectives  41.1 us
    all_gather x1, waiting for transfers between devices, on_device(): conv_part = lax.all_gather(conv_weight, 'hi', axis=2, tiled=True)  40.9 us
    all_gather x1, blocking collectives, on_device(): lax.all_gather(jnp.stack([cluster_id, target]), TOK, axis=1, tiled=True)  37.8 us
    all_gather x1, blocking collectives, on_device(): stats = lax.all_gather(jnp.stack(merge_stats(stats)), TOK)  37 us
    all_gather x1, waiting for transfers between devices, on_device(): gates = lax.all_gather(gate_grads, 'lo', axis=1, tiled=True)  22.6 us
  transfers between devices with their start and end apart: 9, of which 5 were waited for; matrix products, arithmetic and copies ran while one was open for 6% of the time, Pallas kernels for 0%

profile of v1, /device:TPU:0, one launch (start us, length us, event | category | flops | bytes accessed | tf_op | source)
XLA Modules:
  0.0 488.1 jit_solution(5492253558256494669)
XLA Ops:
  9.0 65.8 %all-gather.13.cloned.1.call-done = bf16[2048,512]{1,0:T(8,128)(2,1)} async-done(((bf16[128,512]{1,0:T(8,128)(2,1)}), bf16[2048,512]{1,0:T(8,128)(2,1)}) %all-gather.13.cloned.1.call-update) | async-done | bytes 2097168 | tf_op jit(solution)/shard_map/all_gather | solution.py:83
  76.1 4.4 all-to-all-start
  80.6 55.3 %all-gather.5 = bf16[16,64,16]{1,2,0:T(8,128)(2,1)S(1)} all-gather(bf16[1,64,16]{1,2,0:T(8,128)(2,1)S(1)} %bitcast.207), channel_id=1, replica_groups=mesh['hi'=4,'lo'=4,'ch'=2] {'hi','lo'}, dimensions={0}, use_global_device_ids=true | all-gather | bytes 34816 | tf_op jit(solution)/shard_map/all_gather | solution.py:91
  136.8 37.8 %all_gather.46 = s32[2,2048]{1,0:T(2,128)S(1)} all-gather(s32[2,128]{1,0:T(2,128)S(1)} %pad_add_fusion), channel_id=1, replica_groups=mesh['hi'=4,'lo'=4,'ch'=2] {'hi','lo'}, dimensions={1}, use_global_device_ids=true | all-gather | bytes 17408 | tf_op jit(solution)/shard_map/all_gather | solution.py:85
  177.9 2.9 convolution_convert_fusion.1
  183.4 1.8 all-gather
  187.4 2.1 all-gather.4
  190.3 6.4 %select_reduce_fusion.1 = (f32[2048]{0:T(1024)S(1)}, f32[2048,768]{0,1:T(8,128)S(1)}) fusion(pred[768]{0:T(1024)(128)(4,1)S(1)} %copy-done.18, bf16[2048,1024]{1,0:T(8,128)(2,1)} %all-gather.15.cloned.1.call-done, bf16[1024,112]{1,0:T(8,128)(2,1)S(1)} %broadcast_in_dim.148, bf16[1024,16]{1,0:T(8,128)(2,1)} %bitcast.192, bf16[1024,640]{1,0:T(8,128)(2,1)} %bitcast.26), kind=kOutput, calls=%fused_computation.5 | convolution fusion | flops 3229087744 | bytes 12067584 | tf_op jit(solution)/shard_map/dot_general | solution.py:15
  196.8 2.5 exponential_reduce_fusion
  199.4 1.8 all-gather.6
  201.3 37.0 %all-gather.7 = f32[16,2,2048]{2,1,0:T(2,128)S(1)} all-gather(f32[1,2,2048]{2,1,0:T(2,128)S(1)} %maximum_bitcast_fusion.1), channel_id=5, replica_groups=mesh['hi'=4,'lo'=4,'ch'=2] {'hi','lo'}, dimensions={0}, use_global_device_ids=true | all-gather | bytes 278528 | tf_op jit(solution)/shard_map/all_gather | solution.py:152
  238.8 2.4 subtract_convert_fusion
  241.2 8.5 %convolution_convert_fusion = bf16[2048,1024]{1,0:T(8,128)(2,1)} fusion(bf16[2048,128]{0,1:T(8,128)(2,1)S(1)} %copy-done.10, bf16[2048,768]{0,1:T(8,128)(2,1)S(1)} %subtract_convert_fusion, bf16[1024,128]{1,0:T(8,128)(2,1)S(1)} %copy.69, bf16[1024,112]{1,0:T(8,128)(2,1)S(1)} %broadcast_in_dim.148, bf16[1024,16]{1,0:T(8,128)(2,1)S(1)} %bitcast.193, ...), kind=kOutput, calls=%fused_computation.9 | convolution fusion | flops 3774873600 | bytes 9699328 | tf_op jit(solution)/shard_map/dot_general | solution.py:19
  249.8 10.0 %reduce-scatter.4.cloned.1.call-done = bf16[2048,512]{1,0:T(8,128)(2,1)} async-done(((bf16[2048,1024]{1,0:T(8,128)(2,1)}), bf16[2048,512]{1,0:T(8,128)(2,1)}) %reduce-scatter.4.cloned.1.call-update) | async-done | bytes 2097168 | tf_op jit(solution)/shard_map/reduce_scatter | solution.py:160
  259.9 84.0 %reduce-scatter.6.cloned.1.call-done = bf16[128,512]{1,0:T(8,128)(2,1)} async-done(((bf16[2048,512]{1,0:T(8,128)(2,1)}), bf16[128,512]{1,0:T(8,128)(2,1)}) %reduce-scatter.6.cloned.1.call-update) | async-done | bytes 131088 | tf_op jit(solution)/shard_map/reduce_scatter | solution.py:161
  347.4 22.6 %all-gather.17.cloned.1.call-done = bf16[2,512,512]{2,1,0:T(8,128)(2,1)} async-done(((bf16[2,128,512]{2,1,0:T(8,128)(2,1)}), bf16[2,512,512]{2,1,0:T(8,128)(2,1)}) %all-gather.17.cloned.1.call-update) | async-done | bytes 1048592 | tf_op jit(solution)/shard_map/all_gather | solution.py:173
  376.6 40.9 %all-gather.19.cloned.1.call-done = bf16[2,4,256,512]{3,2,1,0:T(8,128)(2,1)} async-done(((bf16[2,4,64,512]{3,2,1,0:T(8,128)(2,1)}), bf16[2,4,256,512]{3,2,1,0:T(8,128)(2,1)}) %all-gather.19.cloned.1.call-update) | async-done | bytes 2097168 | tf_op jit(solution)/shard_map/all_gather | solution.py:92
  417.5 4.5 fusion.27
  422.1 1.9 copy.71
  423.9 3.7 all-to-all-start.1
  427.9 1.8 all-gather.1
  429.7 41.1 %all-reduce.3 = f32[2048]{0:T(1024)} all-reduce(f32[2048]{0:T(1024)S(1)} %reduce_sum.141), channel_id=7, replica_groups=mesh['hi'=4,'lo'=4,'ch'=2] {'hi','lo'}, use_global_device_ids=true, to_apply=%region_13.14.clone | all-reduce | flops 2048 | bytes 16384
  473.9 1.9 convolution_bitcast_fusion.2
  475.8 2.5 convolution_bitcast_fusion.1
  (138 shorter events, 29.1 us)
Async XLA Ops:
  7.2 174.8 %copy-start = (bf16[1,256,1536]{2,1,0:T(8,128)(2,1)S(1)}, bf16[1,256,1536]{2,1,0:T(8,128)(2,1)}, u32[]{:S(2)}) copy-start(bf16[1,256,1536]{2,1,0:T(8,128)(2,1)} %param.18) | copy-start | bytes 2359300
  7.2 67.7 %copy-start.6 = (bf16[64,10240]{1,0:T(8,128)(2,1)S(1)}, bf16[64,10240]{1,0:T(8,128)(2,1)}, u32[]{:S(2)}) copy-start(bf16[64,10240]{1,0:T(8,128)(2,1)} %param.14) | copy-start | bytes 3932164
  7.2 67.6 %all-gather.13.cloned.1.call-start = ((), (), s32[]{:S(2)}) async-start(), calls=%async_computation.5 | async-start | bytes 2228224 | tf_op jit(solution)/shard_map/all_gather | solution.py:83
  9.0 169.0 %all-gather.15.cloned.1.call-start = ((), (), s32[]{:S(2)}) async-start(), calls=%async_computation.6 | async-start | bytes 6291456 | tf_op jit(solution)/shard_map/all_gather | solution.py:84
  74.8 61.9 %copy-start.25 = (s32[128]{0:T(128)S(1)}, s32[128]{0:T(128)}, u32[]{:S(2)}) copy-start(s32[128]{0:T(128)} %param.21) | copy-start | bytes 1540
  74.9 61.9 %copy-start.26 = (s32[128]{0:T(128)S(1)}, s32[128]{0:T(128)}, u32[]{:S(2)}) copy-start(s32[128]{0:T(128)} %param.20) | copy-start | bytes 1540
  76.1 114.2 %all-to-all-start = ((bf16[64,16,640]{2,0,1:T(8,128)(2,1)}), bf16[64,16,640]{2,0,1:T(8,128)(2,1)}, u32[]{:S(2)}, u32[]{:S(2)}) async-start(bf16[64,16,640]{2,0,1:T(8,128)(2,1)} %bitcast.180), calls=%async_computation | async-start | bytes 2621440 | tf_op jit(solution)/shard_map/all_to_all | solution.py:90
  80.5 100.4 %copy-start.11 = (bf16[1,1024,64]{1,2,0:T(8,128)(2,1)S(1)}, bf16[1,1024,64]{1,2,0:T(8,128)(2,1)}, u32[]{:S(2)}) copy-start(bf16[1,1024,64]{1,2,0:T(8,128)(2,1)} %param.17) | copy-start | bytes 393220
  80.5 100.6 %copy-start.5 = (bf16[1,1024,256]{2,1,0:T(8,128)(2,1)S(1)}, bf16[1,1024,256]{2,1,0:T(8,128)(2,1)}, u32[]{:S(2)}) copy-start(bf16[1,1024,256]{2,1,0:T(8,128)(2,1)} %param.16) | copy-start | bytes 1572868
  80.5 179.3 %reduce-scatter.4.cloned.1.call-start = ((), (), s32[]{:S(2)}) async-start(), calls=%async_computation.7 | async-start | bytes 6291456 | tf_op jit(solution)/shard_map/reduce_scatter | solution.py:160
  176.1 9.6 %copy-start.14 = (s32[1536]{0:T(1024)}, s32[1536]{0:T(1024)S(1)}, u32[]{:S(2)}) copy-start(s32[1536]{0:T(1024)S(1)} %iota_add_fusion.1) | copy-start | bytes 18436
  176.5 9.7 %copy-start.16 = (s32[128]{0:T(128)}, s32[128]{0:T(128)S(1)}, u32[]{:S(2)}) copy-start(s32[128]{0:T(128)S(1)} %get-tuple-element.13) | copy-start | bytes 1540
  177.0 8.7 %copy-start.23 = (pred[128]{0:T(512)(128)(4,1)}, pred[128]{0:T(512)(128)(4,1)S(1)}, u32[]{:S(2)}) copy-start(pred[128]{0:T(512)(128)(4,1)S(1)} %get-tuple-element.30) | copy-start | bytes 388
  189.6 281.3 %copy-start.7 = (bf16[128,320]{1,0:T(8,128)(2,1)}, bf16[128,320]{1,0:T(8,128)(2,1)S(1)}, u32[]{:S(2)}) copy-start(bf16[128,320]{1,0:T(8,128)(2,1)S(1)} %reduce_sum.145) | copy-start | bytes 245764
  196.8 41.9 %copy-start.19 = (pred[768]{0:T(1024)(128)(4,1)S(1)}, pred[768]{0:T(1024)(128)(4,1)}, u32[]{:S(2)}) copy-start(pred[768]{0:T(1024)(128)(4,1)} %iota_compare_fusion.7) | copy-start | bytes 2308
  249.7 94.2 %copy-start.13 = (bf16[2,128,512]{2,1,0:T(8,128)(2,1)S(1)}, bf16[2,128,512]{2,1,0:T(8,128)(2,1)}, u32[]{:S(2)}) copy-start(bf16[2,128,512]{2,1,0:T(8,128)(2,1)} %param.12) | copy-start | bytes 786436
  249.7 96.5 %copy-start.27 = (u32[32]{0:T(128)S(1)}, u32[32]{0:T(128)}, u32[]{:S(2)}) copy-start(u32[32]{0:T(128)} %constant.103) | copy-start | bytes 388
  249.7 94.1 %reduce-scatter.6.cloned.1.call-start = ((), (), s32[]{:S(2)}) async-start(), calls=%async_computation.8 | async-start | bytes 2228224 | tf_op jit(solution)/shard_map/reduce_scatter | solution.py:161
  259.8 110.2 %all-gather.17.cloned.1.call-start = ((), (), s32[]{:S(2)}) async-start(), calls=%async_computation.9 | async-start | bytes 1310720 | tf_op jit(solution)/shard_map/all_gather | solution.py:173
  345.6 71.9 %all-gather.19.cloned.1.call-start = ((), (), s32[]{:S(2)}) async-start(), calls=%async_computation.10 | async-start | bytes 2621440 | tf_op jit(solution)/shard_map/all_gather | solution.py:92
  417.5 10.1 %copy-start.21 = (f32[128]{0:T(128)S(1)}, f32[128]{0:T(128)}, u32[]{:S(2)}) copy-start(f32[128]{0:T(128)} %get-tuple-element.29) | copy-start | bytes 1540
  422.1 53.7 %copy-start.3 = (f32[128,1536]{1,0:T(8,128)S(1)}, f32[128,1536]{1,0:T(8,128)}, u32[]{:S(2)}) copy-start(f32[128,1536]{1,0:T(8,128)} %copy-done.2) | copy-start | bytes 2359300
  423.9 47.8 %all-to-all-start.1 = ((bf16[4,128,256]{1,2,0:T(8,128)(2,1)}), bf16[4,128,256]{1,2,0:T(8,128)(2,1)S(1)}, u32[]{:S(2)}, u32[]{:S(2)}) async-start(bf16[4,128,256]{1,2,0:T(8,128)(2,1)} %copy.71), calls=%async_computation.3 | async-start | bytes 524288 | tf_op jit(solution)/shard_map/all_to_all | solution.py:187
  427.6 52.0 %reduce-scatter.8.cloned.1.call-start = ((), (), s32[]{:S(2)}) async-start(), calls=%async_computation.11 | async-start | bytes 393216 | tf_op jit(solution)/shard_map/reduce_scatter | solution.py:192
  (13 other events, 47.6 us)
Sparse Core Ops, SparseCore 0:
  11.4 63.3 all-gather.12
  76.4 12.3 all-gather.14
  249.8 9.9 reduce-scatter.3
  262.0 81.7 reduce-scatter.5
  346.3 23.7 all-gather.16
  371.6 45.9 all-gather.18
  472.8 3.5 reduce-scatter.7

commit v2 on v1

--- a/solution.py
+++ b/solution.py
@@ -3,7 +3,6 @@
 from jax import lax
 from jax.sharding import Mesh, PartitionSpec as P
 
-K = 4
 LEN = 128
 LANES = 128
 TOK = ("hi", "lo")
@@ -27,6 +26,19 @@
     top = jnp.max(stats[:, 0], axis=0)
     total = jnp.sum(stats[:, 1] * jnp.exp(stats[:, 0] - top), axis=0)
     return top, total
+
+
+def exchange(x, axis):
+    return lax.all_to_all(x, axis, split_axis=0, concat_axis=0, tiled=True)
+
+
+def spread(x, axis):
+    return exchange(jnp.broadcast_to(x[None], (lax.axis_size(axis), *x.shape)), axis)
+
+
+def turned(x, step):
+    groups = lax.axis_size("ch")
+    return lax.ppermute(x, "ch", [(k, (k + step) % groups) for k in range(groups)])
 
 
 def running_count(mine):
@@ -79,16 +91,23 @@
     narrow = model_width // groups
     col_start = ch_index * narrow
 
-    hidden_part = lax.dynamic_slice_in_dim(hidden, col_start, narrow, 1)
-    hidden_cols = lax.all_gather(hidden_part, TOK, axis=0, tiled=True)
-    hidden_all = lax.all_gather(hidden_cols, "ch", axis=1, tiled=True)
-    meta = lax.all_gather(jnp.stack([cluster_id, target]), TOK, axis=1, tiled=True)
-    cluster_all, target_all = meta[0], meta[1]
+    def group_at(step):
+        return lax.rem(ch_index + step + groups, groups) * narrow
+
+    hidden_own = lax.dynamic_slice_in_dim(hidden, col_start, narrow, 1)
+    hidden_own = spread(spread(hidden_own, "hi"), "lo").reshape(tokens, narrow)
+    hidden_by_step = [hidden_own] + [turned(hidden_own, step) for step in range(1, groups)]
+    clusters = cluster_weight.shape[1]
+    share = cluster_weight.shape[0]
+    ids = jnp.stack([cluster_id, target // 256, target % 256]).astype(BF)
+    small = spread(jnp.concatenate([cluster_weight.reshape(-1), ids.reshape(-1)]), TOK)
+    cluster_part = small[:, : share * clusters].reshape(model_width, clusters)
+    ids = small[:, share * clusters :].astype(jnp.int32).reshape(owners // lo, lo, 3, local)
+    ids = ids.transpose(2, 1, 0, 3).reshape(3, tokens)
+    cluster_all, target_all = ids[0], ids[1] * 256 + ids[2]
 
     words = head_weight.shape[1] // owners
-    clusters = cluster_weight.shape[1]
     word_part = lax.all_to_all(head_weight, TOK, split_axis=1, concat_axis=0, tiled=True)
-    cluster_part = lax.all_gather(cluster_weight, TOK, axis=0, tiled=True)
     conv_part = lax.all_gather(conv_weight, "hi", axis=2, tiled=True)
 
     mine = (cluster_all >= 0) & (cluster_all // 2 == me)
@@ -96,7 +115,10 @@
     slot_ids = jnp.where(mine, rank.astype(jnp.int32) - 1, -1)
     chosen = slot_ids[:, None] == jnp.arange(slots, dtype=jnp.int32)[None, :]
     chosen_bf = chosen.astype(BF)
-    rows = t_dot(chosen_bf, hidden_all).astype(BF)
+    rows = jnp.zeros((slots, model_width), BF)
+    for step, part in enumerate(hidden_by_step):
+        picked_part = t_dot(chosen_bf, part).astype(BF)
+        rows = lax.dynamic_update_slice_in_dim(rows, picked_part, group_at(-step), 1)
     word_ids = jnp.sum(jnp.where(chosen, target_all[:, None], 0), axis=0)
     tiers = jnp.sum(jnp.where(chosen, cluster_all[:, None] % 2 + 1, 0), axis=0)
     first_member, second_member = tiers == 1, tiers == 2
@@ -119,9 +141,9 @@
     dz = jnp.sum(lax.all_gather(dz, "ch"), axis=0).astype(BF)
     first_dz = dz[:, : first_proj.shape[1]]
     second_dz = dz[:, first_proj.shape[1] :]
-    back = dot_t(first_dz, first_proj) + dot_t(second_dz, second_proj)
-    col_group = jnp.arange(model_width, dtype=jnp.int32)[None, :] // narrow
-    back = jnp.where(col_group == ch_index, back, 0.0).astype(BF)
+    first_own = lax.dynamic_slice_in_dim(first_proj, col_start, narrow, 0)
+    second_own = lax.dynamic_slice_in_dim(second_proj, col_start, narrow, 0)
+    back = (dot_t(first_dz, first_own) + dot_t(second_dz, second_own)).astype(BF)
     once = jnp.where(ch_index == 0, 1.0, 0.0)
     tail_loss = jnp.where(first_member, once * tail_log[0] - first_pick, 0.0)
     tail_loss = tail_loss + jnp.where(second_member, once * tail_log[1] - second_pick, 0.0)
@@ -137,7 +159,11 @@
     )
     place = jnp.arange(columns.shape[1], dtype=jnp.int32)[None, :]
     limit = jnp.where(me == 0, words + clusters, words)
-    logits = jnp.where(place < limit, dot(hidden_all, columns), -jnp.inf)
+    logits = sum(
+        dot(part, lax.dynamic_slice_in_dim(columns, group_at(-step), narrow, 0))
+        for step, part in enumerate(hidden_by_step)
+    )
+    logits = jnp.where(place < limit, logits, -jnp.inf)
     top = jnp.max(logits, axis=1)
     total = jnp.sum(jnp.exp(logits - top[:, None]), axis=1)
     is_tail = cluster_all >= 0
@@ -149,50 +175,61 @@
     hot = place == jnp.where(is_tail, cluster_place, word_place)[:, None]
     picked = jnp.sum(jnp.where(hot, logits, 0.0), axis=1)
     stats = lax.all_gather(jnp.stack([top, total]), "ch")
-    stats = lax.all_gather(jnp.stack(merge_stats(stats)), TOK)
+    stats = spread(jnp.stack(merge_stats(stats)), TOK)
     top, total = merge_stats(stats)
     head_log = top + jnp.log(total)
+    head_log, conv_part = lax.optimization_barrier((head_log, conv_part))
     slope = (jnp.exp(logits - head_log[:, None]) - hot.astype(F32)).astype(BF)
-    grad_part = dot_t(
-        jnp.concatenate([slope, chosen_bf], axis=1),
-        jnp.concatenate([columns, back.T], axis=1),
-    ).astype(BF)
-    grad_cols = lax.psum_scatter(grad_part, "ch", scatter_dimension=1, tiled=True)
-    grad_sum = lax.psum_scatter(grad_cols, TOK, scatter_dimension=0, tiled=True).astype(F32)
+    grad_sum = 0.0
+    for step in range(1, groups):
+        block = lax.dynamic_slice_in_dim(columns, group_at(step), narrow, 0)
+        grad_sum = grad_sum + turned(dot_t(slope, block).astype(BF), step).astype(F32)
+    block = lax.dynamic_slice_in_dim(columns, col_start, narrow, 0)
+    own_part = dot_t(
+        jnp.concatenate([slope, chosen_bf], axis=1), jnp.concatenate([block, back.T], axis=1)
+    )
+    grad_sum = (grad_sum + own_part).astype(BF).reshape(lo, owners // lo, local, narrow)
+    grad_sum = jnp.sum(exchange(grad_sum, "lo").astype(F32), axis=0).astype(BF)
+    grad_sum = jnp.sum(exchange(grad_sum, "hi").astype(F32), axis=0)
 
     loss_part = jnp.sum(jnp.where(chosen, tail_loss[None, :], 0.0), axis=1) - picked
-    loss_part = jnp.sum(lax.all_gather(loss_part, "ch"), axis=0)
-    own_loss = lax.psum_scatter(loss_part, TOK, scatter_dimension=0, tiled=True)
-    token_loss = own_loss + lax.dynamic_slice_in_dim(head_log, me * local, local, 0)
+    loss_part = loss_part.reshape(lo, owners // lo, local).transpose(1, 0, 2)
+    loss_part = jnp.sum(exchange(loss_part.reshape(owners, local), TOK), axis=0)
+    own_loss = jnp.sum(lax.all_gather(loss_part, "ch"), axis=0)
+    own_log = lax.dynamic_index_in_dim(
+        head_log.reshape(lo, owners // lo, local).transpose(1, 0, 2).reshape(owners, local),
+        me,
+        keepdims=False,
+    )
+    token_loss = own_loss + own_log
 
     gate_a = pre_gates[0].astype(F32)
     gate_sig = jax.nn.sigmoid(pre_gates[1].astype(F32))
     gate_grads = jnp.stack(
         [grad_sum * gate_sig, grad_sum * gate_a * gate_sig * (1.0 - gate_sig)]
     ).astype(BF)
-    gates = lax.all_gather(gate_grads, "lo", axis=1, tiled=True)
-    near = gates.shape[1]
-    blocks = gates.reshape(2, near // LEN, LEN, narrow)
-    shifted = jnp.stack(
-        [
-            jnp.pad(blocks[:, :, offset:], ((0, 0), (0, 0), (0, offset), (0, 0))).reshape(
-                2, near, narrow
-            )
-            for offset in range(K)
-        ]
-    )
-    conv_terms = jnp.einsum(
-        "kgtc,gkrc->tr", shifted, conv_part, preferred_element_type=F32
+    gates = spread(gate_grads, "lo")
+    near = lo * local
+    taps = conv_part.shape[1]
+    reach = conv_part.shape[2]
+    conv_terms = sum(
+        dot_t(gates[:, half].reshape(near, narrow), conv_part[half].reshape(taps * reach, narrow))
+        for half in range(2)
+    ).reshape(near // LEN, LEN, taps * reach)
+    conv_terms = sum(
+        jnp.pad(
+            conv_terms[:, tap:, tap * reach : (tap + 1) * reach], ((0, 0), (0, tap), (0, 0))
+        )
+        for tap in range(taps)
     ).astype(BF)
-    conv_terms = lax.all_to_all(
-        conv_terms.reshape(lo, local, -1), "lo", split_axis=0, concat_axis=0, tiled=True
-    )
-    share = conv_weight.shape[2]
-    conv_terms = conv_terms.reshape(lo, local, -1, share).transpose(1, 2, 0, 3)
-    conv_grad = lax.psum_scatter(
-        conv_terms.reshape(local, model_width), "ch", scatter_dimension=1, tiled=True
-    )
-    grad_input = (grad_sum + conv_grad.astype(F32)).astype(BF)
+    conv_terms = exchange(conv_terms.reshape(lo, local, reach), "lo")
+    conv_terms = conv_terms.reshape(lo, local, owners // lo, share).transpose(1, 2, 0, 3)
+    conv_terms = conv_terms.reshape(local, model_width)
+    conv_grad = lax.dynamic_slice_in_dim(conv_terms, col_start, narrow, 1).astype(F32)
+    for step in range(1, groups):
+        block = lax.dynamic_slice_in_dim(conv_terms, group_at(step), narrow, 1)
+        conv_grad = conv_grad + turned(block, step).astype(F32)
+    grad_input = (grad_sum + conv_grad).astype(BF)
     return (
         token_loss,
         grad_input,

time: 489 us -> 274 us (0.56)
  waiting for transfers between devices: 224 us -> 83.3 us
  blocking collectives: 179 us -> 69.7 us
  starting transfers between devices: 8.29 us -> 36.6 us
  other arithmetic: 15.6 us -> 21.9 us
  local copies, waits for them, and re-layouts: 14.2 us -> 19.1 us
    all_gather x4 -> x1, blocking collectives: 132 us -> 1.76 us  [on_device(): own_loss = jnp.sum(lax.all_gather(loss_part, 'ch'), axis=0)]
    reduce_scatter x3 -> x0, waiting for transfers between devices: 94 us -> none  [the longest x1 84 us: on_device(): lax.psum_scatter(grad_cols, TOK, scatter_dimension=0, tiled=True)]
    all_gather x3 -> x0, waiting for transfers between devices: 88.4 us -> none  [the longest x1 65.8 us: on_device(): hidden_cols = lax.all_gather(hidden_part, TOK, axis=0, tiled=True)]
    all_to_all x0 -> x3, blocking collectives: none -> 61.8 us  [exchange(): return lax.all_to_all(x, axis, split_axis=0, concat_axis=0, tiled=True)]
    unnamed x1 -> x0, blocking collectives: 41.1 us -> none
    all_to_all x1 -> x6, waiting for transfers between devices: 0.01 us -> 41.1 us  [exchange(): return lax.all_to_all(x, axis, split_axis=0, concat_axis=0, tiled=True)]
    all_gather x1, waiting for transfers between devices: 40.9 us -> 0.02 us  [on_device(): conv_part = lax.all_gather(conv_weight, 'hi', axis=2, tiled=True)]
    all_to_all x1, waiting for transfers between devices: 0.01 us -> 40.8 us  [on_device(): lax.all_to_all(head_weight, TOK, split_axis=1, concat_axis=0, tiled=True)]
  transfers between devices with their start and end apart: 9 -> 11, of which waited for: 5 -> 7; matrix products, arithmetic and copies ran while one was open for 6% -> 16% of each run, Pallas kernels for 0% -> 0%
where the time goes in v2:
time: 274 us; the launch traced here: 273 us
  waiting for transfers between devices  83.3 us (30%)
  blocking collectives  69.7 us (25%)
  starting transfers between devices  36.6 us (13%)
  matrix products  27.4 us (10%)
  other arithmetic  21.9 us (8%)
  local copies, waits for them, and re-layouts  19.1 us (7%)
  between operations  14.9 us (5%)
    all_to_all x3, blocking collectives, exchange(): return lax.all_to_all(x, axis, split_axis=0, concat_axis=0, tiled=True)  61.8 us
    all_to_all x6, waiting for transfers between devices, exchange(): return lax.all_to_all(x, axis, split_axis=0, concat_axis=0, tiled=True)  41.1 us
    all_to_all x1, waiting for transfers between devices, on_device(): lax.all_to_all(head_weight, TOK, split_axis=1, concat_axis=0, tiled=True)  40.8 us
    all_to_all x6, starting transfers between devices, exchange(): return lax.all_to_all(x, axis, split_axis=0, concat_axis=0, tiled=True)  32.1 us
    dot_general x8, matrix products, dot_t(): lax.dot_general(a, b, (((1,), (1,)), ((), ())), preferred_element_type=F32)  12.7 us
    unnamed x76, local copies, waits for them, and re-layouts  7.77 us
    dot_general x6, matrix products, t_dot(): lax.dot_general(a, b, (((0,), (0,)), ((), ())), preferred_element_type=F32)  7.42 us
    dot_general x8, matrix products, dot(): return jnp.dot(a, b, preferred_element_type=F32)  7.28 us
  transfers between devices with their start and end apart: 11, of which 7 were waited for; matrix products, arithmetic and copies ran while one was open for 16% of the time, Pallas kernels for 0%

profile of v2, /device:TPU:0, one launch (start us, length us, event | category | flops | bytes accessed | tf_op | source)
XLA Modules:
  0.0 272.9 jit_solution(16910788444283292813)
XLA Ops:
  11.0 8.3 %all-to-all-start = ((bf16[16,2,704]{2,1,0:T(2,128)(2,1)}), bf16[16,2,704]{2,1,0:T(2,128)(2,1)S(1)}, u32[]{:S(2)}, u32[]{:S(2)}) async-start(bf16[16,2,704]{2,1,0:T(2,128)(2,1)} %reshape.287), calls=%async_computation | async-start | bytes 98304 | tf_op jit(solution)/shard_map/all_to_all | solution.py:32
  20.3 6.5 %all-to-all-done = bf16[16,2,704]{2,1,0:T(2,128)(2,1)S(1)} async-done(((bf16[16,2,704]{2,1,0:T(2,128)(2,1)}), bf16[16,2,704]{2,1,0:T(2,128)(2,1)S(1)}, u32[]{:S(2)}, u32[]{:S(2)}) %all-to-all-start) | async-done | bytes 45088 | tf_op jit(solution)/shard_map/all_to_all | solution.py:32
  26.9 15.7 %all_to_all.72 = bf16[4,128,512]{2,1,0:T(8,128)(2,1)S(1)} all-to-all(bf16[4,128,512]{2,1,0:T(8,128)(2,1)S(1)} %broadcast_in_dim.160), channel_id=1, replica_groups=mesh['hi'=4,'lo'=4,'ch'=2] {'hi'}, dimensions={0} | all-to-all | bytes 1048576 | tf_op jit(solution)/shard_map/all_to_all | solution.py:32
  44.1 3.6 %all-to-all-start.2 = ((bf16[4,4,128,512]{3,2,1,0:T(8,128)(2,1)}), bf16[4,4,128,512]{3,2,1,0:T(8,128)(2,1)S(1)}, u32[]{:S(2)}, u32[]{:S(2)}) async-start(bf16[4,4,128,512]{3,2,1,0:T(8,128)(2,1)} %broadcast_in_dim.161), calls=%async_computation.2 | async-start | bytes 4194304 | tf_op jit(solution)/shard_map/all_to_all | solution.py:32
  48.5 2.5 copy.175
  51.1 20.4 %all-to-all-done.2 = bf16[4,4,128,512]{3,2,1,0:T(8,128)(2,1)S(1)} async-done(((bf16[4,4,128,512]{3,2,1,0:T(8,128)(2,1)}), bf16[4,4,128,512]{3,2,1,0:T(8,128)(2,1)S(1)}, u32[]{:S(2)}, u32[]{:S(2)}) %all-to-all-start.2) | async-done | bytes 2097184 | tf_op jit(solution)/shard_map/all_to_all | solution.py:32
  71.5 4.4 %all-to-all-start.3 = ((bf16[64,16,640]{2,0,1:T(8,128)(2,1)}), bf16[64,16,640]{2,0,1:T(8,128)(2,1)}, u32[]{:S(2)}, u32[]{:S(2)}) async-start(bf16[64,16,640]{2,0,1:T(8,128)(2,1)} %bitcast.205), calls=%async_computation.3 | async-start | bytes 2621440 | tf_op jit(solution)/shard_map/all_to_all | solution.py:110
  79.2 40.8 %all-to-all-done.3 = bf16[64,16,640]{2,0,1:T(8,128)(2,1)} async-done(((bf16[64,16,640]{2,0,1:T(8,128)(2,1)}), bf16[64,16,640]{2,0,1:T(8,128)(2,1)}, u32[]{:S(2)}, u32[]{:S(2)}) %all-to-all-start.3) | async-done | bytes 1310752 | tf_op jit(solution)/shard_map/all_to_all | solution.py:110
  124.7 2.1 fusion.11
  130.3 3.7 %fusion.100 = (f32[2048]{0:T(1024)S(1)}, f32[2048,768]{0,1:T(8,128)S(1)}) fusion(f32[2048,768]{0,1:T(8,128)S(1)} %fusion.27, bf16[2048,512]{1,0:T(8,128)(2,1)} %collective-permute-done, bf16[1024,768]{1,0:T(8,128)(2,1)S(1)} %maximum_maximum_fusion, s32[]{:T(128)S(6)} %select_n.150, pred[768]{0:T(1024)(128)(4,1)S(1)} %iota_compare_fusion.8), kind=kOutput, calls=%fused_computation.195 | convolution fusion | flops 1615329280 | bytes 15475716 | tf_op jit(solution)/shard_map/dot_general | solution.py:14
  139.5 8.0 %all-to-all-start.5 = ((f32[16,2,2048]{2,1,0:T(2,128)}), f32[16,2,2048]{2,1,0:T(2,128)}, u32[]{:S(2)}, u32[]{:S(2)}) async-start(f32[16,2,2048]{2,1,0:T(2,128)} %broadcast_in_dim.173), calls=%async_computation.5 | async-start | bytes 524288 | tf_op jit(solution)/shard_map/all_to_all | solution.py:32
  150.7 2.2 fusion.21
  152.9 4.9 %all-to-all-done.5 = f32[16,2,2048]{2,1,0:T(2,128)} async-done(((f32[16,2,2048]{2,1,0:T(2,128)}), f32[16,2,2048]{2,1,0:T(2,128)}, u32[]{:S(2)}, u32[]{:S(2)}) %all-to-all-start.5) | async-done | bytes 262176 | tf_op jit(solution)/shard_map/all_to_all | solution.py:32
  159.3 4.4 %subtract_convert_fusion = bf16[2048,768]{0,1:T(8,128)(2,1)S(1)} fusion(f32[2048,768]{0,1:T(8,128)} %copy-done.2, f32[2048]{0:T(1024)S(1)} %log_add_fusion, s32[2048]{0:T(1024)S(1)} %get-tuple-element.52), kind=kLoop, calls=%fused_computation | loop fusion | flops 7864320 | bytes 9453568 | tf_op jit(solution)/shard_map/convert_element_type | solution.py:182
  163.7 3.3 %convolution_convert_fusion = bf16[2048,512]{1,0:T(8,128)(2,1)} fusion(bf16[2048,768]{0,1:T(8,128)(2,1)S(1)} %subtract_convert_fusion, bf16[1024,768]{1,0:T(8,128)(2,1)S(1)} %copy-done.6, s32[]{:T(128)S(6)} %select_n.164), kind=kOutput, calls=%fused_computation.11 | convolution fusion | flops 1611661312 | bytes 6029316 | tf_op jit(solution)/shard_map/dot_general | solution.py:18
  169.3 2.3 all-gather.3
  172.2 4.9 %add_convert_fusion = bf16[2048,512]{1,0:T(8,128)(2,1)S(1)} fusion(bf16[2048,512]{1,0:T(8,128)(2,1)} %collective-permute-done.1, bf16[2048,128]{0,1:T(8,128)(2,1)S(1)} %copy-done.19, bf16[2048,768]{0,1:T(8,128)(2,1)} %copy-done.10, bf16[512,128]{1,0:T(8,128)(2,1)S(1)} %copy.133, bf16[512,768]{1,0:T(8,128)(2,1)S(1)} %copy-done.16), kind=kOutput, calls=%fused_computation.6 | convolution fusion | flops 1891368960 | bytes 8781824 | tf_op jit(solution)/shard_map/dot_general | solution.py:18
  177.2 28.7 %all_to_all.73 = bf16[4,4,128,512]{3,2,1,0:T(8,128)(2,1)S(1)} all-to-all(bf16[4,4,128,512]{3,2,1,0:T(8,128)(2,1)S(1)} %bitcast.208), channel_id=1, replica_groups=mesh['hi'=4,'lo'=4,'ch'=2] {'lo'}, dimensions={0} | all-to-all | bytes 4194304 | tf_op jit(solution)/shard_map/all_to_all | solution.py:32
  207.1 17.4 %all_to_all.74 = bf16[4,128,512]{2,1,0:T(8,128)(2,1)S(1)} all-to-all(bf16[4,128,512]{2,1,0:T(8,128)(2,1)} %reduce_sum.179), channel_id=1, replica_groups=mesh['hi'=4,'lo'=4,'ch'=2] {'hi'}, dimensions={0} | all-to-all | bytes 1048576 | tf_op jit(solution)/shard_map/all_to_all | solution.py:32
  225.8 3.5 %all-to-all-start.8 = ((bf16[4,2,128,512]{3,2,1,0:T(8,128)(2,1)}), bf16[4,2,128,512]{3,2,1,0:T(8,128)(2,1)S(1)}, u32[]{:S(2)}, u32[]{:S(2)}) async-start(bf16[4,2,128,512]{3,2,1,0:T(8,128)(2,1)} %broadcast_in_dim.176), calls=%async_computation.8 | async-start | bytes 2097152 | tf_op jit(solution)/shard_map/all_to_all | solution.py:32
  234.1 7.9 %all-to-all-done.8 = bf16[4,2,128,512]{3,2,1,0:T(8,128)(2,1)S(1)} async-done(((bf16[4,2,128,512]{3,2,1,0:T(8,128)(2,1)}), bf16[4,2,128,512]{3,2,1,0:T(8,128)(2,1)S(1)}, u32[]{:S(2)}, u32[]{:S(2)}) %all-to-all-start.8) | async-done | bytes 1048608 | tf_op jit(solution)/shard_map/all_to_all | solution.py:32
  242.0 4.5 %all-to-all-start.4 = ((f32[16,1,128]{2,1,0:T(1,128)}), f32[16,1,128]{2,1,0:T(1,128)S(1)}, u32[]{:S(2)}, u32[]{:S(2)}) async-start(f32[16,1,128]{2,1,0:T(1,128)} %bitcast.34), calls=%async_computation.4 | async-start | bytes 16384 | tf_op jit(solution)/shard_map/all_to_all | solution.py:32
  252.1 2.2 add_convert_fusion.1
  254.3 4.1 %all-to-all-start.9 = ((bf16[4,128,256]{1,2,0:T(8,128)(2,1)}), bf16[4,128,256]{1,2,0:T(8,128)(2,1)S(1)}, u32[]{:S(2)}, u32[]{:S(2)}) async-start(bf16[4,128,256]{1,2,0:T(8,128)(2,1)} %add_convert_fusion.1), calls=%async_computation.9 | async-start | bytes 524288 | tf_op jit(solution)/shard_map/all_to_all | solution.py:32
  (180 shorter events, 51.4 us)
Async XLA Ops:
  7.2 120.1 %copy-start = (bf16[1,256,1536]{2,1,0:T(8,128)(2,1)S(1)}, bf16[1,256,1536]{2,1,0:T(8,128)(2,1)}, u32[]{:S(2)}) copy-start(bf16[1,256,1536]{2,1,0:T(8,128)(2,1)} %param.18) | copy-start | bytes 2359300
  11.0 15.8 %all-to-all-start = ((bf16[16,2,704]{2,1,0:T(2,128)(2,1)}), bf16[16,2,704]{2,1,0:T(2,128)(2,1)S(1)}, u32[]{:S(2)}, u32[]{:S(2)}) async-start(bf16[16,2,704]{2,1,0:T(2,128)(2,1)} %reshape.287), calls=%async_computation | async-start | bytes 98304 | tf_op jit(solution)/shard_map/all_to_all | solution.py:32
  44.1 27.4 %all-to-all-start.2 = ((bf16[4,4,128,512]{3,2,1,0:T(8,128)(2,1)}), bf16[4,4,128,512]{3,2,1,0:T(8,128)(2,1)S(1)}, u32[]{:S(2)}, u32[]{:S(2)}) async-start(bf16[4,4,128,512]{3,2,1,0:T(8,128)(2,1)} %broadcast_in_dim.161), calls=%async_computation.2 | async-start | bytes 4194304 | tf_op jit(solution)/shard_map/all_to_all | solution.py:32
  47.7 111.5 %all-gather.8.cloned.1.call-start = ((), (), s32[]{:S(2)}) async-start(), calls=%async_computation.10 | async-start | bytes 2621440 | tf_op jit(solution)/shard_map/all_gather | solution.py:111
  71.5 48.5 %all-to-all-start.3 = ((bf16[64,16,640]{2,0,1:T(8,128)(2,1)}), bf16[64,16,640]{2,0,1:T(8,128)(2,1)}, u32[]{:S(2)}, u32[]{:S(2)}) async-start(bf16[64,16,640]{2,0,1:T(8,128)(2,1)} %bitcast.205), calls=%async_computation.3 | async-start | bytes 2621440 | tf_op jit(solution)/shard_map/all_to_all | solution.py:110
  76.9 47.8 %collective-permute-start = (bf16[2048,512]{1,0:T(8,128)(2,1)S(1)}, bf16[2048,512]{1,0:T(8,128)(2,1)}, u32[]{:S(2)}, u32[]{:S(2)}) collective-permute-start(bf16[2048,512]{1,0:T(8,128)(2,1)S(1)} %bitcast.198), channel_id=1, source_target_pairs={{0,1},{1,0},{2,3},{3,2},{4,5},{5,4},{6,7},{7,6},{8,9},{9,8},{10,11... | collective-permute-start | bytes 6291464 | tf_op jit(solution)/shard_map/ppermute | solution.py:41
  77.2 44.4 %copy-start.29 = (s32[128]{0:T(128)}, s32[128]{0:T(128)S(1)}, u32[]{:S(2)}) copy-start(s32[128]{0:T(128)S(1)} %get-tuple-element.34) | copy-start | bytes 1540
  77.2 89.8 %copy-start.24 = (s32[128]{0:T(128)}, s32[128]{0:T(128)S(1)}, u32[]{:S(2)}) copy-start(s32[128]{0:T(128)S(1)} %get-tuple-element.35) | copy-start | bytes 1540
  121.6 8.7 %copy-start.5 = (bf16[1024,768]{1,0:T(8,128)(2,1)}, bf16[1024,768]{1,0:T(8,128)(2,1)S(1)}, u32[]{:S(2)}) copy-start(bf16[1024,768]{1,0:T(8,128)(2,1)S(1)} %maximum_maximum_fusion) | copy-start | bytes 4718596
  134.1 15.4 %copy-start.28 = (f32[128]{0:T(128)S(1)}, f32[128]{0:T(128)}, u32[]{:S(2)}) copy-start(f32[128]{0:T(128)} %get-tuple-element.33) | copy-start | bytes 1540
  139.5 18.3 %all-to-all-start.5 = ((f32[16,2,2048]{2,1,0:T(2,128)}), f32[16,2,2048]{2,1,0:T(2,128)}, u32[]{:S(2)}, u32[]{:S(2)}) async-start(f32[16,2,2048]{2,1,0:T(2,128)} %broadcast_in_dim.173), calls=%async_computation.5 | async-start | bytes 524288 | tf_op jit(solution)/shard_map/all_to_all | solution.py:32
  150.7 8.4 %copy-start.26 = (f32[128]{0:T(128)}, f32[128]{0:T(128)S(1)}, u32[]{:S(2)}) copy-start(f32[128]{0:T(128)S(1)} %get-tuple-element.55) | copy-start | bytes 1540
  167.0 5.2 %collective-permute-start.1 = (bf16[2048,512]{1,0:T(8,128)(2,1)}, bf16[2048,512]{1,0:T(8,128)(2,1)}, u32[]{:S(2)}, u32[]{:S(2)}) collective-permute-start(bf16[2048,512]{1,0:T(8,128)(2,1)} %convolution_convert_fusion), channel_id=1, source_target_pairs={{0,1},{1,0},{2,3},{3,2},{4,5},{5,4},{6,7},{7,6},{8,9},{9,8},{10,11... | collective-permute-start | bytes 6291464 | tf_op jit(solution)/shard_map/ppermute | solution.py:41
  205.8 18.7 %copy-start.22 = (bf16[2,128,512]{2,1,0:T(8,128)(2,1)S(1)}, bf16[2,128,512]{2,1,0:T(8,128)(2,1)}, u32[]{:S(2)}) copy-start(bf16[2,128,512]{2,1,0:T(8,128)(2,1)} %param.12) | copy-start | bytes 786436
  224.7 6.6 %copy-start.8 = (f32[128,1536]{1,0:T(8,128)S(1)}, f32[128,1536]{1,0:T(8,128)}, u32[]{:S(2)}) copy-start(f32[128,1536]{1,0:T(8,128)} %copy-done.7) | copy-start | bytes 2359300
  224.7 6.6 %copy-start.18 = (bf16[128,256]{1,0:T(8,128)(2,1)S(1)}, bf16[128,256]{1,0:T(8,128)(2,1)}, u32[]{:S(2)}) copy-start(bf16[128,256]{1,0:T(8,128)(2,1)} %copy-done.17) | copy-start | bytes 196612
  224.7 6.6 %copy-start.25 = (s32[128]{0:T(128)S(1)}, s32[128]{0:T(128)}, u32[]{:S(2)}) copy-start(s32[128]{0:T(128)} %copy-done.24) | copy-start | bytes 1540
  224.7 6.6 %copy-start.27 = (f32[128]{0:T(128)S(1)}, f32[128]{0:T(128)}, u32[]{:S(2)}) copy-start(f32[128]{0:T(128)} %copy-done.26) | copy-start | bytes 1540
  225.8 16.2 %all-to-all-start.8 = ((bf16[4,2,128,512]{3,2,1,0:T(8,128)(2,1)}), bf16[4,2,128,512]{3,2,1,0:T(8,128)(2,1)S(1)}, u32[]{:S(2)}, u32[]{:S(2)}) async-start(bf16[4,2,128,512]{3,2,1,0:T(8,128)(2,1)} %broadcast_in_dim.176), calls=%async_computation.8 | async-start | bytes 2097152 | tf_op jit(solution)/shard_map/all_to_all | solution.py:32
  242.0 12.3 %all-to-all-start.4 = ((f32[16,1,128]{2,1,0:T(1,128)}), f32[16,1,128]{2,1,0:T(1,128)S(1)}, u32[]{:S(2)}, u32[]{:S(2)}) async-start(f32[16,1,128]{2,1,0:T(1,128)} %bitcast.34), calls=%async_computation.4 | async-start | bytes 16384 | tf_op jit(solution)/shard_map/all_to_all | solution.py:32
  251.1 8.1 %copy-start.4 = (bf16[128,4608]{1,0:T(8,128)(2,1)S(1)}, bf16[128,4608]{1,0:T(8,128)(2,1)}, u32[]{:S(2)}) copy-start(bf16[128,4608]{1,0:T(8,128)(2,1)} %copy-done.3) | copy-start | bytes 3538948
  254.3 9.5 %all-to-all-start.9 = ((bf16[4,128,256]{1,2,0:T(8,128)(2,1)}), bf16[4,128,256]{1,2,0:T(8,128)(2,1)S(1)}, u32[]{:S(2)}, u32[]{:S(2)}) async-start(bf16[4,128,256]{1,2,0:T(8,128)(2,1)} %add_convert_fusion.1), calls=%async_computation.9 | async-start | bytes 524288 | tf_op jit(solution)/shard_map/all_to_all | solution.py:32
  258.4 7.7 %copy-start.1 = (bf16[1,256,1536]{2,1,0:T(8,128)(2,1)S(1)}, bf16[1,256,1536]{2,1,0:T(8,128)(2,1)}, u32[]{:S(2)}) copy-start(bf16[1,256,1536]{2,1,0:T(8,128)(2,1)} %param.18) | copy-start | bytes 2359300
  263.9 1.4 collective-permute-start.2
  (20 other events, 57.9 us)
Sparse Core Ops, SparseCore 0:
  50.1 67.7 all-gather.7

commit v3 on v2

--- a/solution.py
+++ b/solution.py
@@ -1,6 +1,8 @@
 import jax
 import jax.numpy as jnp
 from jax import lax
+from jax.experimental import pallas as pl
+from jax.experimental.pallas import tpu as pltpu
 from jax.sharding import Mesh, PartitionSpec as P
 
 LEN = 128
@@ -39,6 +41,223 @@
 def turned(x, step):
     groups = lax.axis_size("ch")
     return lax.ppermute(x, "ch", [(k, (k + step) % groups) for k in range(groups)])
+
+
+def around(name, step):
+    size = lax.axis_size(name)
+    return lax.rem(lax.axis_index(name) + (step + size), size)
+
+
+def device(**moved):
+    return {name: moved.get(name, lax.axis_index(name)) for name in ("hi", "lo", "ch")}
+
+
+def tok_device(step):
+    owners, lo = lax.axis_size(TOK), lax.axis_size("lo")
+    me = lax.axis_index("hi") * lo + lax.axis_index("lo")
+    peer = lax.rem(me + step, owners)
+    return peer, device(hi=peer // lo, lo=lax.rem(peer, lo))
+
+
+def greet(peers):
+    barrier = pltpu.get_barrier_semaphore()
+    for peer in peers:
+        pl.semaphore_signal(barrier, inc=1, device_id=peer, device_id_type=pl.DeviceIdType.MESH)
+    pl.semaphore_wait(barrier, len(peers))
+
+
+def push(src, dst, send, recv, peer):
+    copy = pltpu.make_async_remote_copy(
+        src_ref=src,
+        dst_ref=dst,
+        send_sem=send,
+        recv_sem=recv,
+        device_id=peer,
+        device_id_type=pl.DeviceIdType.MESH,
+    )
+    copy.start()
+    return copy
+
+
+def gather_kernel(
+    hidden, small, words, hidden_out, small_out, words_out, hid_s, hid_r, ch_s, ch_r, sm_s, sm_r, w_s, w_r, own
+):
+    owners, his, los = lax.axis_size(TOK), lax.axis_size("hi"), lax.axis_size("lo")
+    groups = lax.axis_size("ch")
+    hi, lo, ch = lax.axis_index("hi"), lax.axis_index("lo"), lax.axis_index("ch")
+    me = hi * los + lo
+    share = words_out.shape[0] // owners
+    width = words_out.shape[1]
+
+    def chunk(peer):
+        if len(words.shape) == 3:
+            return words.at[peer]
+        return words.at[:, pl.ds(pl.multiple_of(peer * width, LANES), width)]
+
+    place = words_out.at[pl.ds(pl.multiple_of(me * share, share), share), :]
+    locals_ = [
+        pltpu.make_async_copy(hidden, hidden_out.at[ch, lo, hi], own.at[0]),
+        pltpu.make_async_copy(small, small_out.at[me], own.at[1]),
+        pltpu.make_async_copy(chunk(me), place, own.at[2]),
+    ]
+    for copy in locals_:
+        copy.start()
+    greet(
+        [tok_device(step)[1] for step in range(1, owners)]
+        + [device(ch=around("ch", step)) for step in range(1, groups)]
+    )
+    ends = []
+    across = {}
+    for a in range(1, his):
+        peer = device(hi=around("hi", a))
+        across[0, a] = push(
+            hidden, hidden_out.at[ch, lo, hi], hid_s.at[0, a], hid_r.at[0, a], peer
+        )
+    for b in range(1, los):
+        peer = device(lo=around("lo", b))
+        across[b, 0] = push(
+            hidden, hidden_out.at[ch, lo, hi], hid_s.at[b, 0], hid_r.at[b, 0], peer
+        )
+    for step in range(1, owners):
+        peer = tok_device(step)[1]
+        ends.append(push(small, small_out.at[me], sm_s.at[step], sm_r.at[step], peer))
+    for step in range(1, owners):
+        index, peer = tok_device(step)
+        ends.append(push(chunk(index), place, w_s.at[step], w_r.at[step], peer))
+    for a in range(1, his):
+        across[0, a].wait_recv()
+        block = hidden_out.at[ch, lo, around("hi", -a)]
+        for b in range(1, los):
+            peer = device(lo=around("lo", b))
+            across[b, a] = push(block, block, hid_s.at[b, a], hid_r.at[b, a], peer)
+    locals_[0].wait()
+    for b in range(los):
+        if b > 0:
+            for a in range(his):
+                across[b, a].wait_recv()
+        block = hidden_out.at[ch, around("lo", -b)]
+        for c in range(1, groups):
+            peer = device(ch=around("ch", c))
+            ends.append(push(block, block, ch_s.at[c, b], ch_r.at[c, b], peer))
+    for copy in across.values():
+        copy.wait_send()
+    for copy in ends + locals_[1:]:
+        copy.wait()
+
+
+def gather(hidden, small, words):
+    owners, his, los = lax.axis_size(TOK), lax.axis_size("hi"), lax.axis_size("lo")
+    groups = lax.axis_size("ch")
+    share = words.shape[0]
+    width = words.shape[1] // owners
+    if width % LANES:
+        words = words.reshape(share, owners, width).transpose(1, 0, 2)
+    dma = pltpu.SemaphoreType.DMA
+    anywhere = pl.BlockSpec(memory_space=pl.ANY)
+    return pl.pallas_call(
+        gather_kernel,
+        out_shape=(
+            jax.ShapeDtypeStruct((groups, los, his, *hidden.shape), BF),
+            jax.ShapeDtypeStruct((owners, *small.shape), BF),
+            jax.ShapeDtypeStruct((owners * share, width), BF),
+        ),
+        in_specs=[anywhere] * 3,
+        out_specs=(anywhere,) * 3,
+        scratch_shapes=[
+            dma((los, his)),
+            dma((los, his)),
+            dma((groups, los)),
+            dma((groups, los)),
+            dma((owners,)),
+            dma((owners,)),
+            dma((owners,)),
+            dma((owners,)),
+            dma((3,)),
+        ],
+        compiler_params=pltpu.CompilerParams(collective_id=0, has_side_effects=True),
+    )(hidden, small, words)
+
+
+def scatter_kernel(
+    grad, gates, sum_out, gates_out, near, mid, far, own_gates, near_s, near_r, far_s, far_r, gate_s, gate_r, own
+):
+    his, los = lax.axis_size("hi"), lax.axis_size("lo")
+    lo = lax.axis_index("lo")
+    hi_peers = [device(hi=around("hi", a)) for a in range(1, his)]
+    lo_peers = [device(lo=around("lo", b)) for b in range(1, los)]
+    greet(hi_peers + lo_peers)
+    order = list(range(1, his)) + [0]
+    copies = {}
+    for a in order:
+        for b in range(1, los):
+            copies[b, a] = push(
+                grad.at[around("lo", b), around("hi", a)],
+                near.at[b, a],
+                near_s.at[b, a],
+                near_r.at[b, a],
+                lo_peers[b - 1],
+            )
+    outward = {}
+    for a in order:
+        total = grad[lo, around("hi", a)].astype(F32)
+        for b in range(1, los):
+            copies[b, a].wait_recv()
+            total = total + near[b, a].astype(F32)
+        if a > 0:
+            mid[a] = total.astype(BF)
+            outward[a] = push(mid.at[a], far.at[a], far_s.at[a], far_r.at[a], hi_peers[a - 1])
+        else:
+            sum_out[...] = total
+    total = sum_out[...]
+    for a in range(1, his):
+        outward[a].wait_recv()
+        total = total + far[a].astype(F32)
+    sum_out[...] = total
+    sig = jax.nn.sigmoid(gates[1].astype(F32))
+    own_gates[0] = (total * sig).astype(BF)
+    own_gates[1] = (total * gates[0].astype(F32) * sig * (1.0 - sig)).astype(BF)
+    spreads = [
+        push(own_gates, gates_out.at[lo], gate_s.at[b], gate_r.at[b], lo_peers[b - 1])
+        for b in range(1, los)
+    ]
+    kept = pltpu.make_async_copy(own_gates, gates_out.at[lo], own)
+    kept.start()
+    for copy in list(copies.values()) + list(outward.values()):
+        copy.wait_send()
+    for copy in spreads:
+        copy.wait()
+    kept.wait()
+
+
+def scatter(grad, gates):
+    los, his, local, narrow = grad.shape
+    dma = pltpu.SemaphoreType.DMA
+    inside = pl.BlockSpec(memory_space=pltpu.VMEM)
+    return pl.pallas_call(
+        scatter_kernel,
+        out_shape=(
+            jax.ShapeDtypeStruct((local, narrow), F32),
+            jax.ShapeDtypeStruct((los, *gates.shape), BF),
+        ),
+        in_specs=[inside] * 2,
+        out_specs=(inside, pl.BlockSpec(memory_space=pl.ANY)),
+        scratch_shapes=[
+            pltpu.VMEM((los, his, local, narrow), BF),
+            pltpu.VMEM((his, local, narrow), BF),
+            pltpu.VMEM((his, local, narrow), BF),
+            pltpu.VMEM(gates.shape, BF),
+            dma((los, his)),
+            dma((los, his)),
+            dma((his,)),
+            dma((his,)),
+            dma((los,)),
+            dma((los,)),
+            dma,
+        ],
+        compiler_params=pltpu.CompilerParams(
+            collective_id=1, has_side_effects=True, vmem_limit_bytes=24 << 20
+        ),
+    )(grad, gates)
 
 
 def running_count(mine):
@@ -95,19 +314,27 @@
         return lax.rem(ch_index + step + groups, groups) * narrow
 
     hidden_own = lax.dynamic_slice_in_dim(hidden, col_start, narrow, 1)
-    hidden_own = spread(spread(hidden_own, "hi"), "lo").reshape(tokens, narrow)
-    hidden_by_step = [hidden_own] + [turned(hidden_own, step) for step in range(1, groups)]
     clusters = cluster_weight.shape[1]
     share = cluster_weight.shape[0]
     ids = jnp.stack([cluster_id, target // 256, target % 256]).astype(BF)
-    small = spread(jnp.concatenate([cluster_weight.reshape(-1), ids.reshape(-1)]), TOK)
+    small = jnp.concatenate([cluster_weight.reshape(-1), ids.reshape(-1)])
+    used = small.shape[0]
+    small = jnp.pad(small, (0, -used % (16 * LANES))).reshape(-1, LANES)
+    hidden_all, small, word_part = gather(hidden_own, small, head_weight)
+    hidden_by_step = [
+        lax.dynamic_index_in_dim(hidden_all, around("ch", -step), keepdims=False).reshape(
+            tokens, narrow
+        )
+        for step in range(groups)
+    ]
+    small = small.reshape(owners, -1)
     cluster_part = small[:, : share * clusters].reshape(model_width, clusters)
-    ids = small[:, share * clusters :].astype(jnp.int32).reshape(owners // lo, lo, 3, local)
+    ids = small[:, share * clusters : used].astype(jnp.int32).reshape(owners // lo, lo, 3, local)
     ids = ids.transpose(2, 1, 0, 3).reshape(3, tokens)
     cluster_all, target_all = ids[0], ids[1] * 256 + ids[2]
 
     words = head_weight.shape[1] // owners
-    word_part = lax.all_to_all(head_weight, TOK, split_axis=1, concat_axis=0, tiled=True)
+    conv_weight, word_part = lax.optimization_barrier((conv_weight, word_part))
     conv_part = lax.all_gather(conv_weight, "hi", axis=2, tiled=True)
 
     mine = (cluster_all >= 0) & (cluster_all // 2 == me)
@@ -189,8 +416,7 @@
         jnp.concatenate([slope, chosen_bf], axis=1), jnp.concatenate([block, back.T], axis=1)
     )
     grad_sum = (grad_sum + own_part).astype(BF).reshape(lo, owners // lo, local, narrow)
-    grad_sum = jnp.sum(exchange(grad_sum, "lo").astype(F32), axis=0).astype(BF)
-    grad_sum = jnp.sum(exchange(grad_sum, "hi").astype(F32), axis=0)
+    grad_sum, gates = scatter(grad_sum, pre_gates)
 
     loss_part = jnp.sum(jnp.where(chosen, tail_loss[None, :], 0.0), axis=1) - picked
     loss_part = loss_part.reshape(lo, owners // lo, local).transpose(1, 0, 2)
@@ -203,12 +429,6 @@
     )
     token_loss = own_loss + own_log
 
-    gate_a = pre_gates[0].astype(F32)
-    gate_sig = jax.nn.sigmoid(pre_gates[1].astype(F32))
-    gate_grads = jnp.stack(
-        [grad_sum * gate_sig, grad_sum * gate_a * gate_sig * (1.0 - gate_sig)]
-    ).astype(BF)
-    gates = spread(gate_grads, "lo")
     near = lo * local
     taps = conv_part.shape[1]
     reach = conv_part.shape[2]

time: 274 us -> 222 us (0.81)
  Pallas kernels: 0 us -> 90.9 us
  blocking collectives: 69.7 us -> 9.67 us
  waiting for transfers between devices: 83.3 us -> 26.9 us
  starting transfers between devices: 36.6 us -> 15.9 us
  other arithmetic: 21.9 us -> 18.4 us
  local copies, waits for them, and re-layouts: 19.1 us -> 16 us
    pallas_call x0 -> x2, Pallas kernels: none -> 90.9 us  [the longest x1 50.5 us: gather(): pl.pallas_call(gather_kernel, out_shape=(jax.ShapeDtypeStruct((groups, lo...]
    all_to_all x3 -> x0, blocking collectives: 61.8 us -> none  [exchange(): return lax.all_to_all(x, axis, split_axis=0, concat_axis=0, tiled=True)]
    all_to_all x6 -> x3, waiting for transfers between devices: 41.1 us -> 0.05 us  [exchange(): return lax.all_to_all(x, axis, split_axis=0, concat_axis=0, tiled=True)]
    all_to_all x1 -> x0, waiting for transfers between devices: 40.8 us -> none  [on_device(): lax.all_to_all(head_weight, TOK, split_axis=1, concat_axis=0, tiled=True)]
    all_gather x1, waiting for transfers between devices: 0.02 us -> 25.6 us  [on_device(): conv_part = lax.all_gather(conv_weight, 'hi', axis=2, tiled=True)]
    all_to_all x6 -> x3, starting transfers between devices: 32.1 us -> 15.6 us  [exchange(): return lax.all_to_all(x, axis, split_axis=0, concat_axis=0, tiled=True)]
    all_to_all x1 -> x0, starting transfers between devices: 4.4 us -> none  [on_device(): lax.all_to_all(head_weight, TOK, split_axis=1, concat_axis=0, tiled=True)]
    broadcast_in_dim x6 -> x1, local copies, waits for them, and re-layouts: 3.97 us -> 0.8 us  [spread(): jnp.broadcast_to(x[None], (lax.axis_size(axis), *x.shape))]
  transfers between devices with their start and end apart: 11 -> 6, of which waited for: 7 -> 2; matrix products, arithmetic and copies ran while one was open for 16% -> 20% of each run, Pallas kernels for 0% -> 18%
where the time goes in v3:
time: 222 us; the launch traced here: 221 us
  Pallas kernels  90.9 us (41%)
  matrix products  28.4 us (13%)
  waiting for transfers between devices  26.9 us (12%)
  other arithmetic  18.4 us (8%)
  local copies, waits for them, and re-layouts  16 us (7%)
  starting transfers between devices  15.9 us (7%)
  between operations  14.8 us (7%)
  blocking collectives  9.67 us (4%)
    pallas_call x1, Pallas kernels, gather(): pl.pallas_call(gather_kernel, out_shape=(jax.ShapeDtypeStruct((groups, lo...  50.5 us
    pallas_call x1, Pallas kernels, scatter(): pl.pallas_call(scatter_kernel, out_shape=(jax.ShapeDtypeStruct((local, na...  40.4 us
    all_gather x1, waiting for transfers between devices, on_device(): conv_part = lax.all_gather(conv_weight, 'hi', axis=2, tiled=True)  25.6 us
    all_to_all x3, starting transfers between devices, exchange(): return lax.all_to_all(x, axis, split_axis=0, concat_axis=0, tiled=True)  15.6 us
    dot_general x8, matrix products, dot_t(): lax.dot_general(a, b, (((1,), (1,)), ((), ())), preferred_element_type=F32)  11.5 us
    unnamed x60, local copies, waits for them, and re-layouts  9.26 us
    dot_general x6, matrix products, t_dot(): lax.dot_general(a, b, (((0,), (0,)), ((), ())), preferred_element_type=F32)  9.13 us
    dot_general x8, matrix products, dot(): return jnp.dot(a, b, preferred_element_type=F32)  7.78 us
  transfers between devices with their start and end apart: 6, of which 2 were waited for; matrix products, arithmetic and copies ran while one was open for 20% of the time, Pallas kernels for 18%

profile of v3, /device:TPU:0, one launch (start us, length us, event | category | flops | bytes accessed | tf_op | source)
XLA Modules:
  0.0 221.1 jit_solution(8839629935027442423)
XLA Ops:
  11.0 50.5 %shard_map.154 = (bf16[2,4,4,128,512]{4,3,2,1,0:T(8,128)(2,1)}, bf16[16,16,128]{2,1,0:T(8,128)(2,1)}, bf16[1024,640]{1,0:T(8,128)(2,1)}) custom-call(bf16[128,512]{1,0:T(8,128)(2,1)} %constant_dynamic-slice_fusion.6.hidden, bf16[16,128]{1,0:T(8,128)(2,1)} %fusion.69.small, bf16[64,10240]{1,0:T(8,128)(2,1)} %words.1), custom_call_target="tpu_custom_call" | custom-call | tf_op jit(solution)/shard_map/pallas_call | solution.py:157
  63.3 2.6 %constant_dynamic-slice_fusion.4 = (bf16[1,4,4,128,512]{4,3,2,1,0:T(8,128)(2,1)S(1)}, bf16[1,4,4,128,512]{4,3,2,1,0:T(8,128)(2,1)S(1)}) fusion(bf16[2,4,4,128,512]{4,3,2,1,0:T(8,128)(2,1)} %get-tuple-element.16, s32[]{:T(128)S(6)} %select_n.158, s32[]{:T(128)S(6)} %select_n.156), kind=kLoop, calls=%fused_computation.145 | loop fusion | bytes 8388616 | tf_op jit(solution)/shard_map/jit(dynamic_index_in_dim)/dynamic_slice | solution.py:325
  66.3 1.9 fusion.27
  68.3 2.1 fusion.102
  70.5 1.6 exponential_reduce_fusion
  73.2 1.9 all-gather.5
  76.0 5.3 %all-to-all-start.1 = ((f32[16,2,2048]{2,1,0:T(2,128)}), f32[16,2,2048]{2,1,0:T(2,128)}, u32[]{:S(2)}, u32[]{:S(2)}) async-start(f32[16,2,2048]{2,1,0:T(2,128)} %broadcast_in_dim.146), calls=%async_computation.1 | async-start | bytes 524288 | tf_op jit(solution)/shard_map/all_to_all | solution.py:34
  82.3 2.1 fusion.12
  87.7 1.6 fusion.100
  90.1 2.0 all-gather
  92.6 1.7 fusion.9
  95.2 1.9 fusion.29
  97.0 6.9 %all-to-all-start = ((f32[16,1,128]{2,1,0:T(1,128)}), f32[16,1,128]{2,1,0:T(1,128)}, u32[]{:S(2)}, u32[]{:S(2)}) async-start(f32[16,1,128]{2,1,0:T(1,128)} %bitcast.34), calls=%async_computation | async-start | bytes 16384 | tf_op jit(solution)/shard_map/all_to_all | solution.py:34
  105.4 25.6 %all-gather.8.cloned.1.call-done = bf16[2,4,256,512]{3,2,1,0:T(8,128)(2,1)} async-done(((bf16[2,4,64,512]{3,2,1,0:T(8,128)(2,1)}), bf16[2,4,256,512]{3,2,1,0:T(8,128)(2,1)}) %all-gather.8.cloned.1.call-update) | async-done | bytes 2097168 | tf_op jit(solution)/shard_map/all_gather | solution.py:338
  131.0 4.3 %subtract_convert_fusion = bf16[2048,768]{0,1:T(8,128)(2,1)S(1)} fusion(f32[2048,768]{0,1:T(8,128)} %copy-done.2, f32[2048]{0:T(1024)S(1)} %log_add_fusion, s32[2048]{0:T(1024)S(1)} %get-tuple-element.48), kind=kLoop, calls=%fused_computation | loop fusion | flops 7864320 | bytes 9453568 | tf_op jit(solution)/shard_map/convert_element_type | solution.py:409
  135.4 3.3 %convolution_convert_fusion = bf16[2048,512]{1,0:T(8,128)(2,1)} fusion(bf16[2048,768]{0,1:T(8,128)(2,1)S(1)} %subtract_convert_fusion, bf16[1024,768]{1,0:T(8,128)(2,1)S(1)} %copy-done.6, s32[]{:T(128)S(6)} %select_n.173), kind=kOutput, calls=%fused_computation.11 | convolution fusion | flops 1611661312 | bytes 6029316 | tf_op jit(solution)/shard_map/dot_general | solution.py:20
  139.2 4.1 %all-gather.3 = f32[256,320]{1,0:T(8,128)} all-gather(f32[128,320]{1,0:T(8,128)S(1)} %pad_maximum_fusion), channel_id=5, replica_groups=mesh['hi'=4,'lo'=4,'ch'=2] {'ch'}, dimensions={0}, use_global_device_ids=true | all-gather | bytes 491520 | tf_op jit(solution)/shard_map/all_gather | solution.py:368
  145.4 2.6 %convolution_bitcast_fusion.1 = f32[1,256,1536]{2,1,0:T(8,128)} fusion(bf16[128,256]{1,0:T(8,128)(2,1)} %copy-done.16, f32[128,1536]{1,0:T(8,128)S(1)} %copy-done.8, f32[128]{0:T(128)S(1)} %copy-done.24, s32[1536]{0:T(1024)S(1)} %iota_add_fusion.1, s32[128]{0:T(128)S(1)} %copy-done.22, pred[128]{0:T(512)(128)(4,1)S(1)} %copy-done.25), kind=kOutput, calls=%fused_computation.14 | convolution fusion | flops 101842944 | bytes 2432128 | tf_op jit(solution)/shard_map/dot_general | solution.py:24
  150.4 4.1 %add_convert_fusion = bf16[2048,512]{1,0:T(8,128)(2,1)S(1)} fusion(bf16[2048,512]{1,0:T(8,128)(2,1)} %collective-permute-done, bf16[2048,128]{0,1:T(8,128)(2,1)S(1)} %fusion.13, bf16[2048,768]{0,1:T(8,128)(2,1)S(1)} %copy-done.10, bf16[512,128]{1,0:T(8,128)(2,1)S(1)} %fusion.10, bf16[512,768]{1,0:T(8,128)(2,1)S(1)} %constant_dynamic-slice_fusion.2), kind=kOutput, calls=%fused_computation.6 | convolution fusion | flops 1891368960 | bytes 8781824 | tf_op jit(solution)/shard_map/dot_general | solution.py:20
  154.5 40.4 %shard_map.155 = (f32[128,512]{1,0:T(8,128)S(1)}, bf16[4,2,128,512]{3,2,1,0:T(8,128)(2,1)S(1)}) custom-call(bf16[4,4,128,512]{3,2,1,0:T(8,128)(2,1)S(1)} %bitcast.184, bf16[2,128,512]{2,1,0:T(8,128)(2,1)S(1)} %copy-done.1), custom_call_target="tpu_custom_call" | custom-call | tf_op jit(solution)/shard_map/pallas_call | solution.py:236
  200.8 2.2 add_convert_fusion.1
  203.0 3.4 %all-to-all-start.2 = ((bf16[4,128,256]{1,2,0:T(8,128)(2,1)}), bf16[4,128,256]{1,2,0:T(8,128)(2,1)S(1)}, u32[]{:S(2)}, u32[]{:S(2)}) async-start(bf16[4,128,256]{1,2,0:T(8,128)(2,1)} %add_convert_fusion.1), calls=%async_computation.2 | async-start | bytes 524288 | tf_op jit(solution)/shard_map/all_to_all | solution.py:34
  206.4 1.6 convolution_bitcast_fusion.3
  210.1 1.8 all-gather.4
  (142 shorter events, 30.8 us)
Async XLA Ops:
  7.2 79.3 %copy-start = (bf16[1,256,1536]{2,1,0:T(8,128)(2,1)S(1)}, bf16[1,256,1536]{2,1,0:T(8,128)(2,1)}, u32[]{:S(2)}) copy-start(bf16[1,256,1536]{2,1,0:T(8,128)(2,1)} %param.18) | copy-start | bytes 2359300
  76.0 21.1 %all-to-all-start.1 = ((f32[16,2,2048]{2,1,0:T(2,128)}), f32[16,2,2048]{2,1,0:T(2,128)}, u32[]{:S(2)}, u32[]{:S(2)}) async-start(f32[16,2,2048]{2,1,0:T(2,128)} %broadcast_in_dim.146), calls=%async_computation.1 | async-start | bytes 524288 | tf_op jit(solution)/shard_map/all_to_all | solution.py:34
  81.3 49.7 %all-gather.8.cloned.1.call-start = ((), (), s32[]{:S(2)}) async-start(), calls=%async_computation.3 | async-start | bytes 2621440 | tf_op jit(solution)/shard_map/all_gather | solution.py:338
  82.3 56.4 %copy-start.21 = (s32[128]{0:T(128)}, s32[128]{0:T(128)S(1)}, u32[]{:S(2)}) copy-start(s32[128]{0:T(128)S(1)} %get-tuple-element.31) | copy-start | bytes 1540
  82.3 3.9 %copy-start.17 = (bf16[1,1024,64]{1,2,0:T(8,128)(2,1)S(1)}, bf16[1,1024,64]{1,2,0:T(8,128)(2,1)}, u32[]{:S(2)}) copy-start(bf16[1,1024,64]{1,2,0:T(8,128)(2,1)} %param.17) | copy-start | bytes 393220
  92.6 46.1 %copy-start.23 = (f32[128]{0:T(128)}, f32[128]{0:T(128)S(1)}, u32[]{:S(2)}) copy-start(f32[128]{0:T(128)S(1)} %get-tuple-element.51) | copy-start | bytes 1540
  97.0 106.0 %all-to-all-start = ((f32[16,1,128]{2,1,0:T(1,128)}), f32[16,1,128]{2,1,0:T(1,128)}, u32[]{:S(2)}, u32[]{:S(2)}) async-start(f32[16,1,128]{2,1,0:T(1,128)} %bitcast.34), calls=%async_computation | async-start | bytes 16384 | tf_op jit(solution)/shard_map/all_to_all | solution.py:34
  105.4 29.9 %copy-start.19 = (f32[2048]{0:T(1024)}, f32[2048]{0:T(1024)S(1)}, u32[]{:S(2)}) copy-start(f32[2048]{0:T(1024)S(1)} %log_add_fusion) | copy-start | bytes 24580
  105.4 29.9 %copy-start.6 = (bf16[1024,768]{1,0:T(8,128)(2,1)S(1)}, bf16[1024,768]{1,0:T(8,128)(2,1)}, u32[]{:S(2)}) copy-start(bf16[1024,768]{1,0:T(8,128)(2,1)} %copy-done.5) | copy-start | bytes 4718596
  135.3 3.3 %copy-start.9 = (bf16[2048,768]{0,1:T(8,128)(2,1)}, bf16[2048,768]{0,1:T(8,128)(2,1)S(1)}, u32[]{:S(2)}) copy-start(bf16[2048,768]{0,1:T(8,128)(2,1)S(1)} %subtract_convert_fusion) | copy-start | bytes 9437188
  135.4 3.3 %copy-start.8 = (f32[128,1536]{1,0:T(8,128)S(1)}, f32[128,1536]{1,0:T(8,128)}, u32[]{:S(2)}) copy-start(f32[128,1536]{1,0:T(8,128)} %copy-done.7) | copy-start | bytes 2359300
  135.4 3.3 %copy-start.25 = (pred[128]{0:T(512)(128)(4,1)S(1)}, pred[128]{0:T(512)(128)(4,1)}, u32[]{:S(2)}) copy-start(pred[128]{0:T(512)(128)(4,1)} %get-tuple-element.54) | copy-start | bytes 388
  138.7 10.1 %collective-permute-start = (bf16[2048,512]{1,0:T(8,128)(2,1)}, bf16[2048,512]{1,0:T(8,128)(2,1)}, u32[]{:S(2)}, u32[]{:S(2)}) collective-permute-start(bf16[2048,512]{1,0:T(8,128)(2,1)} %convolution_convert_fusion), channel_id=1, source_target_pairs={{0,1},{1,0},{2,3},{3,2},{4,5},{5,4},{6,7},{7,6},{8,9},{9,8},{10,11... | collective-permute-start | bytes 6291464 | tf_op jit(solution)/shard_map/ppermute | solution.py:43
  139.1 6.3 %copy-start.22 = (s32[128]{0:T(128)S(1)}, s32[128]{0:T(128)}, u32[]{:S(2)}) copy-start(s32[128]{0:T(128)} %copy-done.21) | copy-start | bytes 1540
  139.1 6.3 %copy-start.24 = (f32[128]{0:T(128)S(1)}, f32[128]{0:T(128)}, u32[]{:S(2)}) copy-start(f32[128]{0:T(128)} %copy-done.23) | copy-start | bytes 1540
  144.3 4.0 %copy-start.15 = (bf16[128,320]{1,0:T(8,128)(2,1)}, bf16[128,320]{1,0:T(8,128)(2,1)S(1)}, u32[]{:S(2)}) copy-start(bf16[128,320]{1,0:T(8,128)(2,1)S(1)} %reduce_sum.155) | copy-start | bytes 245764
  144.3 3.8 %copy-start.18 = (bf16[1,1024,64]{1,2,0:T(8,128)(2,1)S(1)}, bf16[1,1024,64]{1,2,0:T(8,128)(2,1)}, u32[]{:S(2)}) copy-start(bf16[1,1024,64]{1,2,0:T(8,128)(2,1)} %param.17) | copy-start | bytes 393220
  145.4 3.2 %copy-start.11 = (bf16[2,4,256,512]{3,2,1,0:T(8,128)(2,1)S(1)}, bf16[2,4,256,512]{3,2,1,0:T(8,128)(2,1)}, u32[]{:S(2)}) copy-start(bf16[2,4,256,512]{3,2,1,0:T(8,128)(2,1)} %all-gather.8.cloned.1.call-done) | copy-start | bytes 6291460
  148.8 5.7 %copy-start.1 = (bf16[2,128,512]{2,1,0:T(8,128)(2,1)S(1)}, bf16[2,128,512]{2,1,0:T(8,128)(2,1)}, u32[]{:S(2)}) copy-start(bf16[2,128,512]{2,1,0:T(8,128)(2,1)} %gates.1) | copy-start | bytes 786436
  197.7 3.1 %copy-start.12 = (f32[4,128,256]{1,2,0:T(8,128)S(1)}, f32[4,128,256]{1,2,0:T(8,128)}, u32[]{:S(2)}) copy-start(f32[4,128,256]{1,2,0:T(8,128)} %copy.143) | copy-start | bytes 1572868
  199.8 8.3 %copy-start.3 = (bf16[128,4608]{1,0:T(8,128)(2,1)S(1)}, bf16[128,4608]{1,0:T(8,128)(2,1)}, u32[]{:S(2)}) copy-start(bf16[128,4608]{1,0:T(8,128)(2,1)} %fusion.9) | copy-start | bytes 3538948
  200.8 11.1 %copy-start.20 = (f32[2048]{0:T(1024)S(1)}, f32[2048]{0:T(1024)}, u32[]{:S(2)}) copy-start(f32[2048]{0:T(1024)} %copy-done.19) | copy-start | bytes 24580
  203.0 8.9 %all-to-all-start.2 = ((bf16[4,128,256]{1,2,0:T(8,128)(2,1)}), bf16[4,128,256]{1,2,0:T(8,128)(2,1)S(1)}, u32[]{:S(2)}, u32[]{:S(2)}) async-start(bf16[4,128,256]{1,2,0:T(8,128)(2,1)} %add_convert_fusion.1), calls=%async_computation.2 | async-start | bytes 524288 | tf_op jit(solution)/shard_map/all_to_all | solution.py:34
  212.1 1.4 collective-permute-start.1
  (8 other events, 16.2 us)
Sparse Core Ops, SparseCore 0:
  83.7 47.2 all-gather.7

commit v4 on v3

--- a/solution.py
+++ b/solution.py
@@ -179,15 +179,50 @@
 
 
 def scatter_kernel(
-    grad, gates, sum_out, gates_out, near, mid, far, own_gates, near_s, near_r, far_s, far_r, gate_s, gate_r, own
+    grad,
+    gates,
+    conv,
+    loss,
+    sum_out,
+    conv_out,
+    loss_out,
+    near,
+    mid,
+    far,
+    own_gates,
+    all_gates,
+    terms_out,
+    loss_near,
+    loss_mid,
+    loss_far,
+    near_s,
+    near_r,
+    far_s,
+    far_r,
+    gate_s,
+    gate_r,
+    term_s,
+    term_r,
+    ln_s,
+    ln_r,
+    lf_s,
+    lf_r,
+    own,
 ):
     his, los = lax.axis_size("hi"), lax.axis_size("lo")
-    lo = lax.axis_index("lo")
+    hi, lo = lax.axis_index("hi"), lax.axis_index("lo")
     hi_peers = [device(hi=around("hi", a)) for a in range(1, his)]
     lo_peers = [device(lo=around("lo", b)) for b in range(1, los)]
+    local = sum_out.shape[0]
+    reach = conv_out.shape[2]
     greet(hi_peers + lo_peers)
     order = list(range(1, his)) + [0]
     copies = {}
+    ends = []
+    for b in range(1, los):
+        copies["loss", b] = push(
+            loss.at[around("lo", b)], loss_near.at[b], ln_s.at[b], ln_r.at[b], lo_peers[b - 1]
+        )
     for a in order:
         for b in range(1, los):
             copies[b, a] = push(
@@ -198,6 +233,15 @@
                 lo_peers[b - 1],
             )
     outward = {}
+    loss_sum = loss[lo]
+    for b in range(1, los):
+        copies["loss", b].wait_recv()
+        loss_sum = loss_sum + loss_near[b]
+    loss_mid[...] = loss_sum
+    for a in range(1, his):
+        outward["loss", a] = push(
+            loss_mid.at[around("hi", a)], loss_far.at[a], lf_s.at[a], lf_r.at[a], hi_peers[a - 1]
+        )
     for a in order:
         total = grad[lo, around("hi", a)].astype(F32)
         for b in range(1, los):
@@ -208,56 +252,94 @@
             outward[a] = push(mid.at[a], far.at[a], far_s.at[a], far_r.at[a], hi_peers[a - 1])
         else:
             sum_out[...] = total
+    own_loss = loss_mid[hi]
     total = sum_out[...]
     for a in range(1, his):
+        outward["loss", a].wait_recv()
+        own_loss = own_loss + loss_far[a]
         outward[a].wait_recv()
         total = total + far[a].astype(F32)
+    loss_out[...] = own_loss
     sum_out[...] = total
     sig = jax.nn.sigmoid(gates[1].astype(F32))
     own_gates[0] = (total * sig).astype(BF)
     own_gates[1] = (total * gates[0].astype(F32) * sig * (1.0 - sig)).astype(BF)
     spreads = [
-        push(own_gates, gates_out.at[lo], gate_s.at[b], gate_r.at[b], lo_peers[b - 1])
+        push(own_gates, all_gates.at[b], gate_s.at[b], gate_r.at[b], lo_peers[b - 1])
         for b in range(1, los)
     ]
-    kept = pltpu.make_async_copy(own_gates, gates_out.at[lo], own)
-    kept.start()
-    for copy in list(copies.values()) + list(outward.values()):
+    rows = lax.broadcasted_iota(jnp.int32, (local, reach), 0) % LEN
+    for b in range(los):
+        if b > 0:
+            spreads[b - 1].wait_recv()
+            part = all_gates.at[b]
+        else:
+            part = own_gates
+        wide = dot_t(part[0], conv[0]) + dot_t(part[1], conv[1])
+        terms = wide[:, :reach]
+        for tap in range(1, wide.shape[1] // reach):
+            moved = pltpu.roll(wide[:, tap * reach : (tap + 1) * reach], local - tap, 0)
+            terms = terms + jnp.where(rows < LEN - tap, moved, 0.0)
+        terms_out[b] = terms.astype(BF)
+        if b > 0:
+            peer = device(lo=around("lo", -b))
+            ends.append(
+                push(terms_out.at[b], conv_out.at[lo], term_s.at[b], term_r.at[b], peer)
+            )
+        else:
+            kept = pltpu.make_async_copy(terms_out.at[0], conv_out.at[lo], own)
+            kept.start()
+    for copy in list(copies.values()) + list(outward.values()) + spreads:
         copy.wait_send()
-    for copy in spreads:
+    for copy in ends:
         copy.wait()
     kept.wait()
 
 
-def scatter(grad, gates):
+def scatter(grad, gates, conv, loss):
     los, his, local, narrow = grad.shape
+    halves, taps, reach, _ = conv.shape
+    conv = conv.reshape(halves, taps * reach, narrow)
+    loss = jnp.broadcast_to(loss.reshape(los, his, 1, local), (los, his, 8, local))
     dma = pltpu.SemaphoreType.DMA
     inside = pl.BlockSpec(memory_space=pltpu.VMEM)
     return pl.pallas_call(
         scatter_kernel,
         out_shape=(
             jax.ShapeDtypeStruct((local, narrow), F32),
-            jax.ShapeDtypeStruct((los, *gates.shape), BF),
+            jax.ShapeDtypeStruct((los, local, reach), BF),
+            jax.ShapeDtypeStruct((8, local), F32),
         ),
-        in_specs=[inside] * 2,
-        out_specs=(inside, pl.BlockSpec(memory_space=pl.ANY)),
+        in_specs=[inside] * 4,
+        out_specs=(inside, pl.BlockSpec(memory_space=pl.ANY), inside),
         scratch_shapes=[
             pltpu.VMEM((los, his, local, narrow), BF),
             pltpu.VMEM((his, local, narrow), BF),
             pltpu.VMEM((his, local, narrow), BF),
             pltpu.VMEM(gates.shape, BF),
+            pltpu.VMEM((los, *gates.shape), BF),
+            pltpu.VMEM((los, local, reach), BF),
+            pltpu.VMEM((los, his, 8, local), F32),
+            pltpu.VMEM((his, 8, local), F32),
+            pltpu.VMEM((his, 8, local), F32),
             dma((los, his)),
             dma((los, his)),
             dma((his,)),
             dma((his,)),
             dma((los,)),
             dma((los,)),
+            dma((los,)),
+            dma((los,)),
+            dma((los,)),
+            dma((los,)),
+            dma((his,)),
+            dma((his,)),
             dma,
         ],
         compiler_params=pltpu.CompilerParams(
-            collective_id=1, has_side_effects=True, vmem_limit_bytes=24 << 20
+            collective_id=1, has_side_effects=True, vmem_limit_bytes=32 << 20
         ),
-    )(grad, gates)
+    )(grad, gates, conv, loss)
 
 
 def running_count(mine):
@@ -405,7 +487,6 @@
     stats = spread(jnp.stack(merge_stats(stats)), TOK)
     top, total = merge_stats(stats)
     head_log = top + jnp.log(total)
-    head_log, conv_part = lax.optimization_barrier((head_log, conv_part))
     slope = (jnp.exp(logits - head_log[:, None]) - hot.astype(F32)).astype(BF)
     grad_sum = 0.0
     for step in range(1, groups):
@@ -416,12 +497,9 @@
         jnp.concatenate([slope, chosen_bf], axis=1), jnp.concatenate([block, back.T], axis=1)
     )
     grad_sum = (grad_sum + own_part).astype(BF).reshape(lo, owners // lo, local, narrow)
-    grad_sum, gates = scatter(grad_sum, pre_gates)
-
     loss_part = jnp.sum(jnp.where(chosen, tail_loss[None, :], 0.0), axis=1) - picked
-    loss_part = loss_part.reshape(lo, owners // lo, local).transpose(1, 0, 2)
-    loss_part = jnp.sum(exchange(loss_part.reshape(owners, local), TOK), axis=0)
-    own_loss = jnp.sum(lax.all_gather(loss_part, "ch"), axis=0)
+    grad_sum, conv_terms, own_loss = scatter(grad_sum, pre_gates, conv_part, loss_part)
+    own_loss = jnp.sum(lax.all_gather(own_loss[0], "ch"), axis=0)
     own_log = lax.dynamic_index_in_dim(
         head_log.reshape(lo, owners // lo, local).transpose(1, 0, 2).reshape(owners, local),
         me,
@@ -429,20 +507,6 @@
     )
     token_loss = own_loss + own_log
 
-    near = lo * local
-    taps = conv_part.shape[1]
-    reach = conv_part.shape[2]
-    conv_terms = sum(
-        dot_t(gates[:, half].reshape(near, narrow), conv_part[half].reshape(taps * reach, narrow))
-        for half in range(2)
-    ).reshape(near // LEN, LEN, taps * reach)
-    conv_terms = sum(
-        jnp.pad(
-            conv_terms[:, tap:, tap * reach : (tap + 1) * reach], ((0, 0), (0, tap), (0, 0))
-        )
-        for tap in range(taps)
-    ).astype(BF)
-    conv_terms = exchange(conv_terms.reshape(lo, local, reach), "lo")
     conv_terms = conv_terms.reshape(lo, local, owners // lo, share).transpose(1, 2, 0, 3)
     conv_terms = conv_terms.reshape(local, model_width)
     conv_grad = lax.dynamic_slice_in_dim(conv_terms, col_start, narrow, 1).astype(F32)

time: 222 us -> 193 us (0.87)
  waiting for transfers between devices: 26.9 us -> 7.09 us
  starting transfers between devices: 15.9 us -> 5.78 us
  Pallas kernels: 90.9 us -> 97.5 us
  local copies, waits for them, and re-layouts: 16 us -> 12.5 us
  matrix products: 28.4 us -> 25.9 us
  other arithmetic: 18.4 us -> 20.7 us
    all_gather x1, waiting for transfers between devices: 25.6 us -> 5.91 us  [on_device(): conv_part = lax.all_gather(conv_weight, 'hi', axis=2, tiled=True)]
    all_to_all x3 -> x1, starting transfers between devices: 15.6 us -> 5.31 us  [exchange(): return lax.all_to_all(x, axis, split_axis=0, concat_axis=0, tiled=True)]
    pallas_call x1, Pallas kernels: 40.4 us -> 46.9 us  [scatter(): pl.pallas_call(scatter_kernel, out_shape=(jax.ShapeDtypeStruct((local, na...]
    unnamed x60 -> x61, local copies, waits for them, and re-layouts: 9.26 us -> 5.61 us
    dot_general x8 -> x6, matrix products: 11.5 us -> 10.7 us  [dot_t(): lax.dot_general(a, b, (((1,), (1,)), ((), ())), preferred_element_type=F32)]
  transfers between devices with their start and end apart: 6 -> 4, of which waited for: 2 -> 2; matrix products, arithmetic and copies ran while one was open for 20% -> 20% of each run, Pallas kernels for 18% -> 0%
where the time goes in v4:
time: 193 us; the launch traced here: 192 us
  Pallas kernels  97.5 us (51%)
  matrix products  25.9 us (13%)
  other arithmetic  20.7 us (11%)
  between operations  14.7 us (8%)
  local copies, waits for them, and re-layouts  12.5 us (6%)
  blocking collectives  7.99 us (4%)
  waiting for transfers between devices  7.09 us (4%)
  starting transfers between devices  5.78 us (3%)
    pallas_call x1, Pallas kernels, gather(): pl.pallas_call(gather_kernel, out_shape=(jax.ShapeDtypeStruct((groups, lo...  50.5 us
    pallas_call x1, Pallas kernels, scatter(): pl.pallas_call(scatter_kernel, out_shape=(jax.ShapeDtypeStruct((local, na...  46.9 us
    dot_general x6, matrix products, dot_t(): lax.dot_general(a, b, (((1,), (1,)), ((), ())), preferred_element_type=F32)  10.7 us
    dot_general x8, matrix products, dot(): return jnp.dot(a, b, preferred_element_type=F32)  7.8 us
    dot_general x6, matrix products, t_dot(): lax.dot_general(a, b, (((0,), (0,)), ((), ())), preferred_element_type=F32)  7.38 us
    all_gather x1, waiting for transfers between devices, on_device(): conv_part = lax.all_gather(conv_weight, 'hi', axis=2, tiled=True)  5.91 us
    unnamed x61, local copies, waits for them, and re-layouts  5.61 us
    all_to_all x1, starting transfers between devices, exchange(): return lax.all_to_all(x, axis, split_axis=0, concat_axis=0, tiled=True)  5.31 us
  transfers between devices with their start and end apart: 4, of which 2 were waited for; matrix products, arithmetic and copies ran while one was open for 20% of the time, Pallas kernels for 0%

profile of v4, /device:TPU:0, one launch (start us, length us, event | category | flops | bytes accessed | tf_op | source)
XLA Modules:
  0.0 192.1 jit_solution(3100113939847865511)
XLA Ops:
  8.1 1.6 constant_dynamic-slice_fusion.6.hidden
  11.0 50.5 %shard_map.154 = (bf16[2,4,4,128,512]{4,3,2,1,0:T(8,128)(2,1)}, bf16[16,16,128]{2,1,0:T(8,128)(2,1)}, bf16[1024,640]{1,0:T(8,128)(2,1)}) custom-call(bf16[128,512]{1,0:T(8,128)(2,1)} %constant_dynamic-slice_fusion.6.hidden, bf16[16,128]{1,0:T(8,128)(2,1)} %fusion.69.small, bf16[64,10240]{1,0:T(8,128)(2,1)} %words.1), custom_call_target="tpu_custom_call" | custom-call | tf_op jit(solution)/shard_map/pallas_call | solution.py:157
  63.3 2.6 %constant_dynamic-slice_fusion.4 = (bf16[1,4,4,128,512]{4,3,2,1,0:T(8,128)(2,1)S(1)}, bf16[1,4,4,128,512]{4,3,2,1,0:T(8,128)(2,1)S(1)}) fusion(bf16[2,4,4,128,512]{4,3,2,1,0:T(8,128)(2,1)} %get-tuple-element.14, s32[]{:T(128)S(6)} %select_n.153, s32[]{:T(128)S(6)} %select_n.151), kind=kLoop, calls=%fused_computation.144 | loop fusion | bytes 8388616 | tf_op jit(solution)/shard_map/jit(dynamic_index_in_dim)/dynamic_slice | solution.py:407
  66.3 1.9 fusion.27
  68.2 2.1 %fusion.99 = (f32[2048]{0:T(1024)S(1)}, f32[2048,768]{0,1:T(8,128)S(1)}) fusion(f32[2048,768]{0,1:T(8,128)S(1)} %fusion.27, bf16[2048,512]{1,0:T(8,128)(2,1)S(1)} %bitcast.174, bf16[1024,768]{1,0:T(8,128)(2,1)S(1)} %maximum_maximum_fusion, s32[]{:T(128)S(6)} %select_n.154, pred[768]{0:T(1024)(128)(4,1)S(1)} %iota_compare_fusion.9), kind=kOutput, calls=%fused_computation.189 | convolution fusion | flops 1615329280 | bytes 15475716 | tf_op jit(solution)/shard_map/dot_general | solution.py:16
  70.5 1.6 select_reduce_fusion
  73.1 1.9 all-gather.3
  75.9 5.3 %all-to-all-start = ((f32[16,2,2048]{2,1,0:T(2,128)}), f32[16,2,2048]{2,1,0:T(2,128)}, u32[]{:S(2)}, u32[]{:S(2)}) async-start(f32[16,2,2048]{2,1,0:T(2,128)} %broadcast_in_dim.142), calls=%async_computation | async-start | bytes 524288 | tf_op jit(solution)/shard_map/all_to_all | solution.py:34
  82.0 2.1 %fusion.12 = bf16[128,1024]{1,0:T(8,128)(2,1)S(1)} fusion(bf16[128,1024]{1,0:T(8,128)(2,1)S(1)} %broadcast_in_dim.147, s32[]{:T(128)S(6)} %select_n.152, bf16[2048,512]{1,0:T(8,128)(2,1)} %bitcast.177, s32[2048]{0:T(1024)S(1)} %get-tuple-element.43), kind=kOutput, calls=%fused_computation.27 | convolution fusion | flops 268763136 | bytes 2236420 | tf_op jit(solution)/shard_map/dot_general | solution.py:24
  86.8 1.7 fusion.100
  90.4 2.0 %all-gather.1 = f32[4,2,128]{2,1,0:T(2,128)S(1)} all-gather(f32[2,2,128]{2,1,0:T(2,128)S(1)} %copy.99), channel_id=3, replica_groups=mesh['hi'=4,'lo'=4,'ch'=2] {'ch'}, dimensions={0}, use_global_device_ids=true | all-gather | bytes 6144 | tf_op jit(solution)/shard_map/all_gather | solution.py:442
  94.3 2.3 %fusion.8 = bf16[128,4608]{1,0:T(8,128)(2,1)} fusion(f32[128,4608]{1,0:T(8,128)S(1)} %get-tuple-element.55, s32[4608]{0:T(1024)S(1)} %iota_add_fusion, f32[128]{0:T(128)S(1)} %get-tuple-element.46, s32[128]{0:T(128)} %copy-done.20, pred[128]{0:T(512)(128)(4,1)S(1)} %get-tuple-element.49), kind=kLoop, calls=%fused_computation.17 | loop fusion | flops 3538944 | bytes 3558528 | tf_op jit(solution)/shard_map/convert_element_type | solution.py:368
  96.6 1.9 fusion.29
  98.5 1.3 fusion.97
  99.9 4.5 %subtract_convert_fusion = bf16[2048,768]{0,1:T(8,128)(2,1)S(1)} fusion(f32[2048,768]{0,1:T(8,128)} %copy-done.4, s32[2048]{0:T(1024)S(1)} %get-tuple-element.44, f32[2048]{0:T(1024)S(1)} %log_add_fusion), kind=kLoop, calls=%fused_computation.1 | loop fusion | flops 7864320 | bytes 9453568 | tf_op jit(solution)/shard_map/convert_element_type | solution.py:490
  104.4 3.3 %convolution_convert_fusion = bf16[2048,512]{1,0:T(8,128)(2,1)} fusion(bf16[2048,768]{0,1:T(8,128)(2,1)S(1)} %subtract_convert_fusion, bf16[1024,768]{1,0:T(8,128)(2,1)S(1)} %copy-done.8, s32[]{:T(128)S(6)} %select_n.159), kind=kOutput, calls=%fused_computation.11 | convolution fusion | flops 1611661312 | bytes 6029316 | tf_op jit(solution)/shard_map/dot_general | solution.py:20
  109.9 2.4 %all-gather.2 = f32[256,320]{1,0:T(8,128)} all-gather(f32[128,320]{1,0:T(8,128)S(1)} %pad_maximum_fusion), channel_id=4, replica_groups=mesh['hi'=4,'lo'=4,'ch'=2] {'ch'}, dimensions={0}, use_global_device_ids=true | all-gather | bytes 491520 | tf_op jit(solution)/shard_map/all_gather | solution.py:450
  116.9 1.6 convolution_bitcast_fusion.1
  118.5 1.3 convolution_bitcast_fusion
  120.8 4.1 %add_convert_fusion = bf16[2048,512]{1,0:T(8,128)(2,1)S(1)} fusion(bf16[2048,512]{1,0:T(8,128)(2,1)} %collective-permute-done, bf16[2048,128]{0,1:T(8,128)(2,1)S(1)} %fusion.13, bf16[2048,768]{0,1:T(8,128)(2,1)S(1)} %copy-done.12, bf16[512,128]{1,0:T(8,128)(2,1)S(1)} %fusion.10, bf16[512,768]{1,0:T(8,128)(2,1)S(1)} %constant_dynamic-slice_fusion.3), kind=kOutput, calls=%fused_computation.6 | convolution fusion | flops 1891368960 | bytes 8781824 | tf_op jit(solution)/shard_map/dot_general | solution.py:20
  124.9 5.9 %all-gather.7.cloned.1.call-done = bf16[2,4,256,512]{3,2,1,0:T(8,128)(2,1)} async-done(((bf16[2,4,64,512]{3,2,1,0:T(8,128)(2,1)}), bf16[2,4,256,512]{3,2,1,0:T(8,128)(2,1)}) %all-gather.7.cloned.1.call-update) | async-done | bytes 2097168 | tf_op jit(solution)/shard_map/all_gather | solution.py:420
  130.8 1.6 copy-done.1
  132.4 46.9 %shard_map.155 = (f32[128,512]{1,0:T(8,128)S(1)}, bf16[4,128,256]{2,1,0:T(8,128)(2,1)S(1)}, f32[8,128]{1,0:T(8,128)S(1)}) custom-call(bf16[4,4,128,512]{3,2,1,0:T(8,128)(2,1)S(1)} %bitcast.173, bf16[2,128,512]{2,1,0:T(8,128)(2,1)S(1)} %copy-done.2, bf16[2,1024,512]{2,1,0:T(8,128)(2,1)S(1)} %bitcast.172, f32[4,4,8,128]{3,2,1,0:T(8,128)S(1)} %broadcast_in_dim.157.loss), custom_call_target="tpu_custom_call" | custom-call | tf_op jit(solution)/shard_map/pallas_call | solution.py:306
  180.1 1.8 all-gather.4
  (130 shorter events, 25.3 us)
Async XLA Ops:
  7.2 81.3 %copy-start = (bf16[1,256,1536]{2,1,0:T(8,128)(2,1)S(1)}, bf16[1,256,1536]{2,1,0:T(8,128)(2,1)}, u32[]{:S(2)}) copy-start(bf16[1,256,1536]{2,1,0:T(8,128)(2,1)} %param.18) | copy-start | bytes 2359300
  63.3 2.6 %copy-start.13 = (bf16[1024,640]{1,0:T(8,128)(2,1)S(1)}, bf16[1024,640]{1,0:T(8,128)(2,1)}, u32[]{:S(2)}) copy-start(bf16[1024,640]{1,0:T(8,128)(2,1)} %get-tuple-element.16) | copy-start | bytes 3932164
  65.9 2.3 %copy-start.6 = (bf16[1,4,4,128,512]{4,3,2,1,0:T(8,128)(2,1)}, bf16[1,4,4,128,512]{4,3,2,1,0:T(8,128)(2,1)S(1)}, u32[]{:S(2)}) copy-start(bf16[1,4,4,128,512]{4,3,2,1,0:T(8,128)(2,1)S(1)} %get-tuple-element.31) | copy-start | bytes 6291460
  70.4 2.7 %copy-start.4 = (f32[2048,768]{0,1:T(8,128)}, f32[2048,768]{0,1:T(8,128)S(1)}, u32[]{:S(2)}) copy-start(f32[2048,768]{0,1:T(8,128)S(1)} %get-tuple-element.53) | copy-start | bytes 18874372
  75.9 22.6 %all-to-all-start = ((f32[16,2,2048]{2,1,0:T(2,128)}), f32[16,2,2048]{2,1,0:T(2,128)}, u32[]{:S(2)}, u32[]{:S(2)}) async-start(f32[16,2,2048]{2,1,0:T(2,128)} %broadcast_in_dim.142), calls=%async_computation | async-start | bytes 524288 | tf_op jit(solution)/shard_map/all_to_all | solution.py:34
  81.2 49.6 %all-gather.7.cloned.1.call-start = ((), (), s32[]{:S(2)}) async-start(), calls=%async_computation.1 | async-start | bytes 2621440 | tf_op jit(solution)/shard_map/all_gather | solution.py:420
  81.9 3.4 %copy-start.17 = (bf16[1,1024,64]{1,2,0:T(8,128)(2,1)S(1)}, bf16[1,1024,64]{1,2,0:T(8,128)(2,1)}, u32[]{:S(2)}) copy-start(bf16[1,1024,64]{1,2,0:T(8,128)(2,1)} %param.17) | copy-start | bytes 393220
  85.3 4.8 %copy-start.20 = (s32[128]{0:T(128)}, s32[128]{0:T(128)S(1)}, u32[]{:S(2)}) copy-start(s32[128]{0:T(128)S(1)} %get-tuple-element.29) | copy-start | bytes 1540
  86.8 3.3 %copy-start.15 = (bf16[128,256]{1,0:T(8,128)(2,1)}, bf16[128,256]{1,0:T(8,128)(2,1)S(1)}, u32[]{:S(2)}) copy-start(bf16[128,256]{1,0:T(8,128)(2,1)S(1)} %convolution_convert_fusion.3) | copy-start | bytes 196612
  88.5 4.0 %copy-start.25 = (s32[128]{0:T(128)S(1)}, s32[128]{0:T(128)}, u32[]{:S(2)}) copy-start(s32[128]{0:T(128)} %get-tuple-element.28) | copy-start | bytes 1540
  99.9 4.5 %copy-start.8 = (bf16[1024,768]{1,0:T(8,128)(2,1)S(1)}, bf16[1024,768]{1,0:T(8,128)(2,1)}, u32[]{:S(2)}) copy-start(bf16[1024,768]{1,0:T(8,128)(2,1)} %copy-done.7) | copy-start | bytes 4718596
  104.4 3.3 %copy-start.11 = (bf16[2048,768]{0,1:T(8,128)(2,1)}, bf16[2048,768]{0,1:T(8,128)(2,1)S(1)}, u32[]{:S(2)}) copy-start(bf16[2048,768]{0,1:T(8,128)(2,1)S(1)} %subtract_convert_fusion) | copy-start | bytes 9437188
  104.4 3.5 %copy-start.10 = (f32[128,1536]{1,0:T(8,128)S(1)}, f32[128,1536]{1,0:T(8,128)}, u32[]{:S(2)}) copy-start(f32[128,1536]{1,0:T(8,128)} %copy-done.9) | copy-start | bytes 2359300
  104.4 3.5 %copy-start.21 = (s32[128]{0:T(128)S(1)}, s32[128]{0:T(128)}, u32[]{:S(2)}) copy-start(s32[128]{0:T(128)} %copy-done.20) | copy-start | bytes 1540
  104.4 3.5 %copy-start.23 = (f32[128]{0:T(128)S(1)}, f32[128]{0:T(128)}, u32[]{:S(2)}) copy-start(f32[128]{0:T(128)} %get-tuple-element.47) | copy-start | bytes 1540
  104.4 3.5 %copy-start.26 = (pred[128]{0:T(512)(128)(4,1)S(1)}, pred[128]{0:T(512)(128)(4,1)}, u32[]{:S(2)}) copy-start(pred[128]{0:T(512)(128)(4,1)} %get-tuple-element.48) | copy-start | bytes 388
  107.7 12.7 %collective-permute-start = (bf16[2048,512]{1,0:T(8,128)(2,1)}, bf16[2048,512]{1,0:T(8,128)(2,1)}, u32[]{:S(2)}, u32[]{:S(2)}) collective-permute-start(bf16[2048,512]{1,0:T(8,128)(2,1)} %convolution_convert_fusion), channel_id=1, source_target_pairs={{0,1},{1,0},{2,3},{3,2},{4,5},{5,4},{6,7},{7,6},{8,9},{9,8},{10,11... | collective-permute-start | bytes 6291464 | tf_op jit(solution)/shard_map/ppermute | solution.py:43
  115.7 2.8 %copy-start.5 = (bf16[128,4608]{1,0:T(8,128)(2,1)S(1)}, bf16[128,4608]{1,0:T(8,128)(2,1)}, u32[]{:S(2)}) copy-start(bf16[128,4608]{1,0:T(8,128)(2,1)} %fusion.8) | copy-start | bytes 3538948
  116.9 3.0 %copy-start.18 = (bf16[1,1024,64]{1,2,0:T(8,128)(2,1)S(1)}, bf16[1,1024,64]{1,2,0:T(8,128)(2,1)}, u32[]{:S(2)}) copy-start(bf16[1,1024,64]{1,2,0:T(8,128)(2,1)} %param.17) | copy-start | bytes 393220
  116.9 3.2 %copy-start.14 = (bf16[1,1024,256]{2,1,0:T(8,128)(2,1)S(1)}, bf16[1,1024,256]{2,1,0:T(8,128)(2,1)}, u32[]{:S(2)}) copy-start(bf16[1,1024,256]{2,1,0:T(8,128)(2,1)} %param.16) | copy-start | bytes 1572868
  118.5 2.3 %copy-start.12 = (bf16[2048,768]{0,1:T(8,128)(2,1)S(1)}, bf16[2048,768]{0,1:T(8,128)(2,1)}, u32[]{:S(2)}) copy-start(bf16[2048,768]{0,1:T(8,128)(2,1)} %copy-done.11) | copy-start | bytes 9437188
  120.4 10.4 %copy-start.19 = (f32[2048]{0:T(1024)S(1)}, f32[2048]{0:T(1024)}, u32[]{:S(2)}) copy-start(f32[2048]{0:T(1024)} %sub.177) | copy-start | bytes 24580
  120.4 10.4 %copy-start.2 = (bf16[2,128,512]{2,1,0:T(8,128)(2,1)S(1)}, bf16[2,128,512]{2,1,0:T(8,128)(2,1)}, u32[]{:S(2)}) copy-start(bf16[2,128,512]{2,1,0:T(8,128)(2,1)} %gates.1) | copy-start | bytes 786436
  183.1 1.4 collective-permute-start.1
  (8 other events, 13.4 us)
Sparse Core Ops, SparseCore 0:
  83.6 47.1 all-gather.6

commit v5 on v4

--- a/solution.py
+++ b/solution.py
@@ -84,7 +84,7 @@
 ):
     owners, his, los = lax.axis_size(TOK), lax.axis_size("hi"), lax.axis_size("lo")
     groups = lax.axis_size("ch")
-    hi, lo, ch = lax.axis_index("hi"), lax.axis_index("lo"), lax.axis_index("ch")
+    hi, lo = lax.axis_index("hi"), lax.axis_index("lo")
     me = hi * los + lo
     share = words_out.shape[0] // owners
     width = words_out.shape[1]
@@ -96,7 +96,7 @@
 
     place = words_out.at[pl.ds(pl.multiple_of(me * share, share), share), :]
     locals_ = [
-        pltpu.make_async_copy(hidden, hidden_out.at[ch, lo, hi], own.at[0]),
+        pltpu.make_async_copy(hidden, hidden_out.at[0, lo, hi], own.at[0]),
         pltpu.make_async_copy(small, small_out.at[me], own.at[1]),
         pltpu.make_async_copy(chunk(me), place, own.at[2]),
     ]
@@ -111,12 +111,12 @@
     for a in range(1, his):
         peer = device(hi=around("hi", a))
         across[0, a] = push(
-            hidden, hidden_out.at[ch, lo, hi], hid_s.at[0, a], hid_r.at[0, a], peer
+            hidden, hidden_out.at[0, lo, hi], hid_s.at[0, a], hid_r.at[0, a], peer
         )
     for b in range(1, los):
         peer = device(lo=around("lo", b))
         across[b, 0] = push(
-            hidden, hidden_out.at[ch, lo, hi], hid_s.at[b, 0], hid_r.at[b, 0], peer
+            hidden, hidden_out.at[0, lo, hi], hid_s.at[b, 0], hid_r.at[b, 0], peer
         )
     for step in range(1, owners):
         peer = tok_device(step)[1]
@@ -126,7 +126,7 @@
         ends.append(push(chunk(index), place, w_s.at[step], w_r.at[step], peer))
     for a in range(1, his):
         across[0, a].wait_recv()
-        block = hidden_out.at[ch, lo, around("hi", -a)]
+        block = hidden_out.at[0, lo, around("hi", -a)]
         for b in range(1, los):
             peer = device(lo=around("lo", b))
             across[b, a] = push(block, block, hid_s.at[b, a], hid_r.at[b, a], peer)
@@ -135,10 +135,11 @@
         if b > 0:
             for a in range(his):
                 across[b, a].wait_recv()
-        block = hidden_out.at[ch, around("lo", -b)]
+        block = hidden_out.at[0, around("lo", -b)]
         for c in range(1, groups):
             peer = device(ch=around("ch", c))
-            ends.append(push(block, block, ch_s.at[c, b], ch_r.at[c, b], peer))
+            there = hidden_out.at[c, around("lo", -b)]
+            ends.append(push(block, there, ch_s.at[c, b], ch_r.at[c, b], peer))
     for copy in across.values():
         copy.wait_send()
     for copy in ends + locals_[1:]:
@@ -181,7 +182,7 @@
 def scatter_kernel(
     grad,
     gates,
-    conv,
+    conv_all,
     loss,
     sum_out,
     conv_out,
@@ -208,7 +209,11 @@
     lf_s,
     lf_r,
     own,
+    conv,
+    conv_sem,
 ):
+    conv_copy = pltpu.make_async_copy(conv_all, conv, conv_sem)
+    conv_copy.start()
     his, los = lax.axis_size("hi"), lax.axis_size("lo")
     hi, lo = lax.axis_index("hi"), lax.axis_index("lo")
     hi_peers = [device(hi=around("hi", a)) for a in range(1, his)]
@@ -269,6 +274,7 @@
         for b in range(1, los)
     ]
     rows = lax.broadcasted_iota(jnp.int32, (local, reach), 0) % LEN
+    conv_copy.wait()
     for b in range(los):
         if b > 0:
             spreads[b - 1].wait_recv()
@@ -310,7 +316,7 @@
             jax.ShapeDtypeStruct((los, local, reach), BF),
             jax.ShapeDtypeStruct((8, local), F32),
         ),
-        in_specs=[inside] * 4,
+        in_specs=[inside, inside, pl.BlockSpec(memory_space=pl.ANY), inside],
         out_specs=(inside, pl.BlockSpec(memory_space=pl.ANY), inside),
         scratch_shapes=[
             pltpu.VMEM((los, his, local, narrow), BF),
@@ -335,6 +341,8 @@
             dma((his,)),
             dma((his,)),
             dma,
+            pltpu.VMEM(conv.shape, BF),
+            dma,
         ],
         compiler_params=pltpu.CompilerParams(
             collective_id=1, has_side_effects=True, vmem_limit_bytes=32 << 20
@@ -403,12 +411,7 @@
     used = small.shape[0]
     small = jnp.pad(small, (0, -used % (16 * LANES))).reshape(-1, LANES)
     hidden_all, small, word_part = gather(hidden_own, small, head_weight)
-    hidden_by_step = [
-        lax.dynamic_index_in_dim(hidden_all, around("ch", -step), keepdims=False).reshape(
-            tokens, narrow
-        )
-        for step in range(groups)
-    ]
+    hidden_by_step = [hidden_all[step].reshape(tokens, narrow) for step in range(groups)]
     small = small.reshape(owners, -1)
     cluster_part = small[:, : share * clusters].reshape(model_width, clusters)
     ids = small[:, share * clusters : used].astype(jnp.int32).reshape(owners // lo, lo, 3, local)

time: 193 us -> 196 us (1.016)
    slice x0 -> x1, local copies, waits for them, and re-layouts: none -> 4.01 us  [on_device(): hidden_all[step].reshape(tokens, narrow)]
    dynamic_slice x1 -> x0, local copies, waits for them, and re-layouts: 2.63 us -> none  [on_device(): lax.dynamic_index_in_dim(hidden_all, around('ch', -step), keepdims=False)]
    unnamed x61 -> x59, local copies, waits for them, and re-layouts: 5.61 us -> 5.81 us
where the time goes in v5:
time: 196 us; the launch traced here: 195 us
  Pallas kernels  97.7 us (50%)
  matrix products  25.9 us (13%)
  other arithmetic  22.1 us (11%)
  between operations  14.7 us (8%)
  local copies, waits for them, and re-layouts  14 us (7%)
  blocking collectives  7.99 us (4%)
  waiting for transfers between devices  7.1 us (4%)
  starting transfers between devices  5.8 us (3%)
    pallas_call x1, Pallas kernels, gather(): pl.pallas_call(gather_kernel, out_shape=(jax.ShapeDtypeStruct((groups, lo...  50.5 us
    pallas_call x1, Pallas kernels, scatter(): pl.pallas_call(scatter_kernel, out_shape=(jax.ShapeDtypeStruct((local, na...  47.1 us
    dot_general x6, matrix products, dot_t(): lax.dot_general(a, b, (((1,), (1,)), ((), ())), preferred_element_type=F32)  10.7 us
    dot_general x8, matrix products, dot(): return jnp.dot(a, b, preferred_element_type=F32)  7.79 us
    dot_general x6, matrix products, t_dot(): lax.dot_general(a, b, (((0,), (0,)), ((), ())), preferred_element_type=F32)  7.38 us
    all_gather x1, waiting for transfers between devices, on_device(): conv_part = lax.all_gather(conv_weight, 'hi', axis=2, tiled=True)  5.92 us
    unnamed x59, local copies, waits for them, and re-layouts  5.81 us
    all_to_all x1, starting transfers between devices, exchange(): return lax.all_to_all(x, axis, split_axis=0, concat_axis=0, tiled=True)  5.31 us
  transfers between devices with their start and end apart: 4, of which 2 were waited for; matrix products, arithmetic and copies ran while one was open for 20% of the time, Pallas kernels for 0%

profile of v5, /device:TPU:0, one launch (start us, length us, event | category | flops | bytes accessed | tf_op | source)
XLA Modules:
  0.0 195.2 jit_solution(3133571232059672647)
XLA Ops:
  8.1 1.6 constant_dynamic-slice_fusion.4.hidden
  11.0 50.5 %shard_map.154 = (bf16[2,4,4,128,512]{4,3,2,1,0:T(8,128)(2,1)}, bf16[16,16,128]{2,1,0:T(8,128)(2,1)}, bf16[1024,640]{1,0:T(8,128)(2,1)}) custom-call(bf16[128,512]{1,0:T(8,128)(2,1)} %constant_dynamic-slice_fusion.4.hidden, bf16[16,128]{1,0:T(8,128)(2,1)} %fusion.69.small, bf16[64,10240]{1,0:T(8,128)(2,1)} %words.1), custom_call_target="tpu_custom_call" | custom-call | tf_op jit(solution)/shard_map/pallas_call | solution.py:158
  62.5 4.0 %fusion.97 = (bf16[1,4,4,128,512]{4,3,2,1,0:T(8,128)(2,1)S(1)}, bf16[1,4,4,128,512]{4,3,2,1,0:T(8,128)(2,1)}) fusion(bf16[2,4,4,128,512]{4,3,2,1,0:T(8,128)(2,1)} %get-tuple-element.14), kind=kLoop, calls=%fused_computation.185 | loop fusion | bytes 8388608 | tf_op jit(solution)/shard_map/slice | solution.py:414
  67.3 1.8 maximum_maximum_fusion
  69.3 1.9 fusion.27
  71.2 2.1 %fusion.100 = (f32[2048]{0:T(1024)S(1)}, f32[2048,768]{0,1:T(8,128)S(1)}) fusion(f32[2048,768]{0,1:T(8,128)S(1)} %fusion.27, bf16[2048,512]{1,0:T(8,128)(2,1)S(1)} %bitcast.174, bf16[1024,768]{1,0:T(8,128)(2,1)S(1)} %maximum_maximum_fusion, s32[]{:T(128)S(6)} %select_n.145, pred[768]{0:T(1024)(128)(4,1)S(1)} %iota_compare_fusion.9), kind=kOutput, calls=%fused_computation.188 | convolution fusion | flops 1615329280 | bytes 15475716 | tf_op jit(solution)/shard_map/dot_general | solution.py:16
  73.4 1.6 select_reduce_fusion
  76.0 1.9 all-gather.3
  78.8 5.3 %all-to-all-start = ((f32[16,2,2048]{2,1,0:T(2,128)}), f32[16,2,2048]{2,1,0:T(2,128)}, u32[]{:S(2)}, u32[]{:S(2)}) async-start(f32[16,2,2048]{2,1,0:T(2,128)} %broadcast_in_dim.142), calls=%async_computation | async-start | bytes 524288 | tf_op jit(solution)/shard_map/all_to_all | solution.py:34
  84.9 2.1 %fusion.12 = bf16[128,1024]{1,0:T(8,128)(2,1)S(1)} fusion(bf16[128,1024]{1,0:T(8,128)(2,1)S(1)} %broadcast_in_dim.147, s32[]{:T(128)S(6)} %select_n.144, bf16[2048,512]{1,0:T(8,128)(2,1)} %bitcast.176, s32[2048]{0:T(1024)S(1)} %get-tuple-element.43), kind=kOutput, calls=%fused_computation.27 | convolution fusion | flops 268763136 | bytes 2236420 | tf_op jit(solution)/shard_map/dot_general | solution.py:24
  89.8 1.7 fusion.101
  93.4 2.0 %all-gather.1 = f32[4,2,128]{2,1,0:T(2,128)S(1)} all-gather(f32[2,2,128]{2,1,0:T(2,128)S(1)} %copy.99), channel_id=3, replica_groups=mesh['hi'=4,'lo'=4,'ch'=2] {'ch'}, dimensions={0}, use_global_device_ids=true | all-gather | bytes 6144 | tf_op jit(solution)/shard_map/all_gather | solution.py:445
  97.2 2.3 %fusion.8 = bf16[128,4608]{1,0:T(8,128)(2,1)} fusion(f32[128,4608]{1,0:T(8,128)S(1)} %get-tuple-element.55, s32[4608]{0:T(1024)S(1)} %iota_add_fusion, f32[128]{0:T(128)S(1)} %get-tuple-element.46, s32[128]{0:T(128)} %copy-done.19, pred[128]{0:T(512)(128)(4,1)S(1)} %get-tuple-element.49), kind=kLoop, calls=%fused_computation.17 | loop fusion | flops 3538944 | bytes 3558528 | tf_op jit(solution)/shard_map/convert_element_type | solution.py:376
  99.5 1.9 fusion.29
  101.4 1.3 fusion.98
  102.9 4.5 %subtract_convert_fusion = bf16[2048,768]{0,1:T(8,128)(2,1)S(1)} fusion(f32[2048,768]{0,1:T(8,128)} %copy-done.4, s32[2048]{0:T(1024)S(1)} %get-tuple-element.44, f32[2048]{0:T(1024)S(1)} %log_add_fusion), kind=kLoop, calls=%fused_computation.1 | loop fusion | flops 7864320 | bytes 9453568 | tf_op jit(solution)/shard_map/convert_element_type | solution.py:493
  107.4 3.3 %convolution_convert_fusion = bf16[2048,512]{1,0:T(8,128)(2,1)} fusion(bf16[2048,768]{0,1:T(8,128)(2,1)S(1)} %subtract_convert_fusion, bf16[1024,768]{1,0:T(8,128)(2,1)S(1)} %copy-done.8, s32[]{:T(128)S(6)} %select_n.150), kind=kOutput, calls=%fused_computation.11 | convolution fusion | flops 1611661312 | bytes 6029316 | tf_op jit(solution)/shard_map/dot_general | solution.py:20
  112.9 2.4 %all-gather.2 = f32[256,320]{1,0:T(8,128)} all-gather(f32[128,320]{1,0:T(8,128)S(1)} %pad_maximum_fusion), channel_id=4, replica_groups=mesh['hi'=4,'lo'=4,'ch'=2] {'ch'}, dimensions={0}, use_global_device_ids=true | all-gather | bytes 491520 | tf_op jit(solution)/shard_map/all_gather | solution.py:453
  119.8 1.6 convolution_bitcast_fusion.1
  123.8 4.1 %add_convert_fusion = bf16[2048,512]{1,0:T(8,128)(2,1)S(1)} fusion(bf16[2048,512]{1,0:T(8,128)(2,1)} %collective-permute-done, bf16[2048,128]{0,1:T(8,128)(2,1)S(1)} %fusion.13, bf16[2048,768]{0,1:T(8,128)(2,1)S(1)} %copy-done.12, bf16[512,128]{1,0:T(8,128)(2,1)S(1)} %fusion.10, bf16[512,768]{1,0:T(8,128)(2,1)S(1)} %constant_dynamic-slice_fusion.3), kind=kOutput, calls=%fused_computation.6 | convolution fusion | flops 1891368960 | bytes 8781824 | tf_op jit(solution)/shard_map/dot_general | solution.py:20
  127.9 5.9 %all-gather.7.cloned.1.call-done = bf16[2,4,256,512]{3,2,1,0:T(8,128)(2,1)} async-done(((bf16[2,4,64,512]{3,2,1,0:T(8,128)(2,1)}), bf16[2,4,256,512]{3,2,1,0:T(8,128)(2,1)}) %all-gather.7.cloned.1.call-update) | async-done | bytes 2097168 | tf_op jit(solution)/shard_map/all_gather | solution.py:423
  133.8 1.6 copy-done.1
  135.4 47.1 %shard_map.155 = (f32[128,512]{1,0:T(8,128)S(1)}, bf16[4,128,256]{2,1,0:T(8,128)(2,1)S(1)}, f32[8,128]{1,0:T(8,128)S(1)}) custom-call(bf16[4,4,128,512]{3,2,1,0:T(8,128)(2,1)S(1)} %bitcast.173, bf16[2,128,512]{2,1,0:T(8,128)(2,1)S(1)} %copy-done.2, bf16[2,1024,512]{2,1,0:T(8,128)(2,1)S(1)} %bitcast.172, f32[4,4,8,128]{3,2,1,0:T(8,128)S(1)} %broadcast_in_dim.157.loss), custom_call_target="tpu_custom_call" | custom-call | tf_op jit(solution)/shard_map/pallas_call | solution.py:312
  183.2 1.8 all-gather.4
  (128 shorter events, 26.4 us)
Async XLA Ops:
  7.2 84.3 %copy-start = (bf16[1,256,1536]{2,1,0:T(8,128)(2,1)S(1)}, bf16[1,256,1536]{2,1,0:T(8,128)(2,1)}, u32[]{:S(2)}) copy-start(bf16[1,256,1536]{2,1,0:T(8,128)(2,1)} %param.18) | copy-start | bytes 2359300
  69.1 2.1 %copy-start.7 = (bf16[1024,768]{1,0:T(8,128)(2,1)}, bf16[1024,768]{1,0:T(8,128)(2,1)S(1)}, u32[]{:S(2)}) copy-start(bf16[1024,768]{1,0:T(8,128)(2,1)S(1)} %maximum_maximum_fusion) | copy-start | bytes 4718596
  73.3 2.7 %copy-start.4 = (f32[2048,768]{0,1:T(8,128)}, f32[2048,768]{0,1:T(8,128)S(1)}, u32[]{:S(2)}) copy-start(f32[2048,768]{0,1:T(8,128)S(1)} %get-tuple-element.53) | copy-start | bytes 18874372
  78.8 22.6 %all-to-all-start = ((f32[16,2,2048]{2,1,0:T(2,128)}), f32[16,2,2048]{2,1,0:T(2,128)}, u32[]{:S(2)}, u32[]{:S(2)}) async-start(f32[16,2,2048]{2,1,0:T(2,128)} %broadcast_in_dim.142), calls=%async_computation | async-start | bytes 524288 | tf_op jit(solution)/shard_map/all_to_all | solution.py:34
  84.1 49.6 %all-gather.7.cloned.1.call-start = ((), (), s32[]{:S(2)}) async-start(), calls=%async_computation.1 | async-start | bytes 2621440 | tf_op jit(solution)/shard_map/all_gather | solution.py:423
  84.9 3.4 %copy-start.16 = (bf16[1,1024,64]{1,2,0:T(8,128)(2,1)S(1)}, bf16[1,1024,64]{1,2,0:T(8,128)(2,1)}, u32[]{:S(2)}) copy-start(bf16[1,1024,64]{1,2,0:T(8,128)(2,1)} %param.17) | copy-start | bytes 393220
  88.3 4.8 %copy-start.19 = (s32[128]{0:T(128)}, s32[128]{0:T(128)S(1)}, u32[]{:S(2)}) copy-start(s32[128]{0:T(128)S(1)} %get-tuple-element.29) | copy-start | bytes 1540
  89.8 3.2 %copy-start.14 = (bf16[128,256]{1,0:T(8,128)(2,1)}, bf16[128,256]{1,0:T(8,128)(2,1)S(1)}, u32[]{:S(2)}) copy-start(bf16[128,256]{1,0:T(8,128)(2,1)S(1)} %convolution_convert_fusion.3) | copy-start | bytes 196612
  91.4 4.0 %copy-start.24 = (s32[128]{0:T(128)S(1)}, s32[128]{0:T(128)}, u32[]{:S(2)}) copy-start(s32[128]{0:T(128)} %get-tuple-element.28) | copy-start | bytes 1540
  102.9 4.5 %copy-start.8 = (bf16[1024,768]{1,0:T(8,128)(2,1)S(1)}, bf16[1024,768]{1,0:T(8,128)(2,1)}, u32[]{:S(2)}) copy-start(bf16[1024,768]{1,0:T(8,128)(2,1)} %copy-done.7) | copy-start | bytes 4718596
  107.4 3.3 %copy-start.11 = (bf16[2048,768]{0,1:T(8,128)(2,1)}, bf16[2048,768]{0,1:T(8,128)(2,1)S(1)}, u32[]{:S(2)}) copy-start(bf16[2048,768]{0,1:T(8,128)(2,1)S(1)} %subtract_convert_fusion) | copy-start | bytes 9437188
  107.4 3.5 %copy-start.10 = (f32[128,1536]{1,0:T(8,128)S(1)}, f32[128,1536]{1,0:T(8,128)}, u32[]{:S(2)}) copy-start(f32[128,1536]{1,0:T(8,128)} %copy-done.9) | copy-start | bytes 2359300
  107.4 3.5 %copy-start.20 = (s32[128]{0:T(128)S(1)}, s32[128]{0:T(128)}, u32[]{:S(2)}) copy-start(s32[128]{0:T(128)} %copy-done.19) | copy-start | bytes 1540
  107.4 3.5 %copy-start.22 = (f32[128]{0:T(128)S(1)}, f32[128]{0:T(128)}, u32[]{:S(2)}) copy-start(f32[128]{0:T(128)} %get-tuple-element.47) | copy-start | bytes 1540
  107.4 3.5 %copy-start.25 = (pred[128]{0:T(512)(128)(4,1)S(1)}, pred[128]{0:T(512)(128)(4,1)}, u32[]{:S(2)}) copy-start(pred[128]{0:T(512)(128)(4,1)} %get-tuple-element.48) | copy-start | bytes 388
  110.7 12.7 %collective-permute-start = (bf16[2048,512]{1,0:T(8,128)(2,1)}, bf16[2048,512]{1,0:T(8,128)(2,1)}, u32[]{:S(2)}, u32[]{:S(2)}) collective-permute-start(bf16[2048,512]{1,0:T(8,128)(2,1)} %convolution_convert_fusion), channel_id=1, source_target_pairs={{0,1},{1,0},{2,3},{3,2},{4,5},{5,4},{6,7},{7,6},{8,9},{9,8},{10,11... | collective-permute-start | bytes 6291464 | tf_op jit(solution)/shard_map/ppermute | solution.py:43
  117.8 2.0 %copy-start.26 = (pred[128]{0:T(512)(128)(4,1)S(1)}, pred[128]{0:T(512)(128)(4,1)}, u32[]{:S(2)}) copy-start(pred[128]{0:T(512)(128)(4,1)} %get-tuple-element.48) | copy-start | bytes 388
  118.7 2.8 %copy-start.5 = (bf16[128,4608]{1,0:T(8,128)(2,1)S(1)}, bf16[128,4608]{1,0:T(8,128)(2,1)}, u32[]{:S(2)}) copy-start(bf16[128,4608]{1,0:T(8,128)(2,1)} %fusion.8) | copy-start | bytes 3538948
  119.8 3.0 %copy-start.17 = (bf16[1,1024,64]{1,2,0:T(8,128)(2,1)S(1)}, bf16[1,1024,64]{1,2,0:T(8,128)(2,1)}, u32[]{:S(2)}) copy-start(bf16[1,1024,64]{1,2,0:T(8,128)(2,1)} %param.17) | copy-start | bytes 393220
  119.8 3.2 %copy-start.13 = (bf16[1,1024,256]{2,1,0:T(8,128)(2,1)S(1)}, bf16[1,1024,256]{2,1,0:T(8,128)(2,1)}, u32[]{:S(2)}) copy-start(bf16[1,1024,256]{2,1,0:T(8,128)(2,1)} %param.16) | copy-start | bytes 1572868
  121.5 2.3 %copy-start.12 = (bf16[2048,768]{0,1:T(8,128)(2,1)S(1)}, bf16[2048,768]{0,1:T(8,128)(2,1)}, u32[]{:S(2)}) copy-start(bf16[2048,768]{0,1:T(8,128)(2,1)} %copy-done.11) | copy-start | bytes 9437188
  123.4 10.4 %copy-start.18 = (f32[2048]{0:T(1024)S(1)}, f32[2048]{0:T(1024)}, u32[]{:S(2)}) copy-start(f32[2048]{0:T(1024)} %sub.177) | copy-start | bytes 24580
  123.4 10.4 %copy-start.2 = (bf16[2,128,512]{2,1,0:T(8,128)(2,1)S(1)}, bf16[2,128,512]{2,1,0:T(8,128)(2,1)}, u32[]{:S(2)}) copy-start(bf16[2,128,512]{2,1,0:T(8,128)(2,1)} %gates.1) | copy-start | bytes 786436
  186.3 1.4 collective-permute-start.1
  (7 other events, 11.5 us)
Sparse Core Ops, SparseCore 0:
  86.5 47.1 all-gather.6
